TPU v7x, 512 devices: a whole 4x8x8 slice. The times are simulated.
512 devices in a mesh: gx: 32 (over z_lo, y), gy: 4 (over z_hi, core), gz: 4 (over x).
Axes of the slice: x: 4, y: 8, z: 8 (z_hi: 2, z_lo: 4; z = z_hi * 4 + z_lo), core: 2. Of those that a mesh axis runs over, the one named last changes fastest.
Arguments:
- displacement: float32 [3, 768, 128, 512], P(None, 'gx', 'gy', 'gz'), may hold values from -40 to 40, as said below
- density: float32 [768, 128, 512], P('gx', 'gy', 'gz'), may hold values from 0.05 to 1
Outputs:
- sensitivity: float32 [768, 128, 512], P('gx', 'gy', 'gz')
- mean_energy: float32 [], replicated
Inputs may be any that keep to these rules, and one draw needn't show every extreme that they name: `displacement`: displacements of the stored nodes.
All inputs are finite; a program needn't handle non-finite values.
Results may differ from a plain program's by a relative error of at most 0.0001.
Values sent between devices are 32-bit elements; how exact they have to be, the bound alone decides.
A program may use at most 64 MiB of HBM per device.

v0:
```python
import jax
import jax.numpy as jnp
import numpy as np
from jax import lax
from jax.sharding import PartitionSpec as P

HAT = (1.0, 2.0, 3.0, 2.0, 1.0)


def extended_2(block, sides, width):
    for axis, dim in sides:
        count = lax.axis_size(axis)
        forward = [(i, i + 1) for i in range(count - 1)]
        backward = [(target, source) for source, target in forward]
        low = lax.ppermute(
            lax.slice_in_dim(block, block.shape[dim] - width, None, axis=dim), axis, forward
        )
        high = lax.ppermute(lax.slice_in_dim(block, 0, width, axis=dim), axis, backward)
        block = jnp.concatenate([low, block, high], axis=dim)
    return block


def passed_along(block, axis, distance):
    devices = range(lax.axis_size(axis))
    route = [(i - distance, i) for i in devices if i - distance in devices]
    return lax.ppermute(block, axis, route)


def brick_stiffness():
    ratio = 0.3
    lame_first = ratio / ((1.0 + ratio) * (1.0 - 2.0 * ratio))
    shear = 1.0 / (2.0 * (1.0 + ratio))
    elastic = np.zeros((6, 6))
    elastic[:3, :3] = lame_first
    for index in range(3):
        elastic[index, index] += 2.0 * shear
        elastic[index + 3, index + 3] = shear
    point = 1.0 / np.sqrt(3.0)
    result = np.zeros((24, 24))
    for first in (-point, point):
        for second in (-point, point):
            for third in (-point, point):
                strain_map = np.zeros((6, 24))
                for corner in range(8):
                    signs = [2 * (corner // 4) - 1, 2 * (corner // 2 % 2) - 1, 2 * (corner % 2) - 1]
                    along_x = signs[0] * (1 + signs[1] * second) * (1 + signs[2] * third) / 4.0
                    along_y = signs[1] * (1 + signs[0] * first) * (1 + signs[2] * third) / 4.0
                    along_z = signs[2] * (1 + signs[0] * first) * (1 + signs[1] * second) / 4.0
                    base = 3 * corner
                    strain_map[0, base] = along_x
                    strain_map[1, base + 1] = along_y
                    strain_map[2, base + 2] = along_z
                    strain_map[3, base] = along_y
                    strain_map[3, base + 1] = along_x
                    strain_map[4, base + 1] = along_z
                    strain_map[4, base + 2] = along_y
                    strain_map[5, base] = along_z
                    strain_map[5, base + 2] = along_x
                result += strain_map.T @ elastic @ strain_map / 8.0
    return result


def hat_valid(padded, dim, count):
    total = HAT[0] * lax.slice_in_dim(padded, 0, count, axis=dim)
    for offset in range(1, 5):
        total = total + HAT[offset] * lax.slice_in_dim(padded, offset, offset + count, axis=dim)
    return total


def coverage(count, start, extent):
    positions = start + jnp.arange(count, dtype=jnp.int32)
    total = jnp.zeros((count,), jnp.float32)
    for offset in range(5):
        near = positions + (offset - 2)
        inside = (near >= 0) & (near < extent)
        total = total + jnp.where(inside, jnp.float32(HAT[offset]), jnp.float32(0.0))
    return total


def element_energy(low, high, stiffness):
    rows = low.shape[2] - 1
    depth = low.shape[3]

    def slab(index):
        lows = lax.dynamic_slice_in_dim(low, index, 2, 1)
        highs = lax.dynamic_slice_in_dim(high, index, 2, 1)
        corners = []
        for corner in range(8):
            source = highs if corner % 2 else lows
            shift_y = corner // 2 % 2
            corners.append(source[:, corner // 4, shift_y : shift_y + rows, :])
        vector = jnp.stack(corners, 0).reshape(24, rows * depth)
        image = jnp.dot(stiffness, vector, precision=lax.Precision.HIGHEST)
        return jnp.sum(vector * image, 0).reshape(rows, depth)

    return lax.map(slab, jnp.arange(low.shape[1] - 1, dtype=jnp.int32))


def smooth(field):
    size_x, size_y, size_z = field.shape
    padded = extended_2(field, (("gx", 0), ("gy", 1), ("gz", 2)), 2)
    return hat_valid(hat_valid(hat_valid(padded, 0, size_x), 1, size_y), 2, size_z)


def shards(displacement, density):
    size_x, size_y, size_z = density.shape
    stiffness = jnp.asarray(brick_stiffness(), jnp.float32)
    cover_x = coverage(size_x, lax.axis_index("gx") * size_x, size_x * lax.axis_size("gx"))
    cover_y = coverage(size_y, lax.axis_index("gy") * size_y, size_y * lax.axis_size("gy"))
    cover_z = coverage(size_z, lax.axis_index("gz") * size_z, size_z * lax.axis_size("gz"))
    normal = cover_x[:, None, None] * cover_y[None, :, None] * cover_z[None, None, :]
    physical = smooth(density) / normal
    face_x = passed_along(displacement[:, 0], "gx", -1)
    extended = jnp.concatenate([displacement, face_x[:, None]], 1)
    face_y = passed_along(extended[:, :, 0], "gy", -1)
    extended = jnp.concatenate([extended, face_y[:, :, None]], 2)
    face_z = passed_along(extended[:, :, :, 0], "gz", -1)
    upper = jnp.concatenate([extended[..., 1:], face_z[..., None]], 3)
    energy = element_energy(extended, upper, stiffness)
    local_total = jnp.sum(physical**3 * energy)
    total = lax.psum(local_total, ("gx", "gy", "gz"))
    element_count = (
        size_x * size_y * size_z * lax.axis_size("gx") * lax.axis_size("gy") * lax.axis_size("gz")
    )
    mean_energy = total / element_count
    slope = -3.0 * physical**2 * energy
    sensitivity = smooth(slope / normal) / mean_energy
    return (sensitivity, mean_energy)


def solution(mesh):
    return jax.shard_map(
        shards,
        mesh=mesh,
        in_specs=(P(None, "gx", "gy", "gz"), P("gx", "gy", "gz")),
        out_specs=(P("gx", "gy", "gz"), P()),
        check_vma=False,
    )
```

profile of v0, /device:TPU:1, one launch (start us, length us, event | category | flops | bytes accessed | tf_op | source)
XLA Modules:
  0.0 388.9 jit_solution(14195358618377111354)
XLA Ops:
  3.6 4.6 %collective-permute-start = (f32[2,32,128]{2,1,0:T(8,128)S(1)}, f32[2,32,128]{2,1,0:T(8,128)S(1)}, u32[]{:S(2)}, u32[]{:S(2)}) collective-permute-start(f32[2,32,128]{2,1,0:T(8,128)S(1)} %get-tuple-element.124), channel_id=1, source_target_pairs={{0,16},{16,32},{32,48},{48,64},{64,80},{80,96},{96,112},{112,128},... | collective-permute-start | bytes 98312 | tf_op jit(solution)/shard_map/ppermute | solution.py:15
  12.9 13.1 %collective-permute-start.2 = (f32[28,2,128]{2,0,1:T(8,128)S(1)}, f32[28,2,128]{2,0,1:T(8,128)S(1)}, u32[]{:S(2)}, u32[]{:S(2)}) collective-permute-start(f32[28,2,128]{2,0,1:T(8,128)S(1)} %copy.103), channel_id=1, source_target_pairs={{0,4},{4,8},{8,12},{1,5},{5,9},{9,13},{2,6},{6,10},{10,14},{3,7},{... | collective-permute-start | bytes 86024 | tf_op jit(solution)/shard_map/ppermute | solution.py:15
  28.0 2.8 copy.84
  30.8 2.6 dynamic-update-slice.9
  33.4 2.9 copy.83
  36.3 2.9 copy.85
  40.3 3.4 collective-permute-start.4
  64.0 2.6 copy.90
  66.6 4.2 %pad_maximum_fusion = (f32[3,25,33,128]{3,1,0,2:T(8,128)}, f32[3,25,33,128]{3,1,0,2:T(8,128)}) fusion(f32[3,25,1,128]{3,1,0,2:T(8,128)S(1)} %bitcast.80, f32[3,25,32,128]{3,1,0,2:T(8,128)S(1)} %dynamic-update-slice.9, f32[3,25,33,1]{3,1,0,2:T(8,128)} %copy.90, f32[3,25,33,127]{3,1,0,2:T(8,128)} %fusion.11), kind=kLoop, calls=%fused_computation.31 | loop fusion | flops 633600 | bytes 5068800 | tf_op jit(solution)/shard_map/concatenate | solution.py:116
  70.8 159.1 %while.11 = (s32[]{:T(128)}, f32[24,32,128]{2,1,0:T(8,128)}, s32[24]{0:T(128)S(1)}, f32[3,25,33,128]{3,1,0,2:T(8,128)}, f32[3,25,33,128]{3,1,0,2:T(8,128)}, /*in...) while((s32[]{:T(128)}, f32[24,32,128]{2,1,0:T(8,128)}, s32[24]{0:T(128)S(1)}, ...), condition=%wide.region_2.3_spmd.clone, body=%wide.region_0.2_spmd.sunk.clone.sunk | while | flops 28504072 | bytes 2018231 | solution.py:96
  73.3 2.8 constant_dynamic-slice_fusion.9
  80.1 2.8 constant_dynamic-slice_fusion.9
  87.0 2.8 constant_dynamic-slice_fusion.9
  93.8 2.8 constant_dynamic-slice_fusion.9
  100.7 2.8 constant_dynamic-slice_fusion.9
  107.5 2.8 constant_dynamic-slice_fusion.9
  114.3 2.8 constant_dynamic-slice_fusion.9
  179.5 2.6 constant_dynamic-slice_fusion.9
  186.2 2.6 constant_dynamic-slice_fusion.9
  192.8 2.6 constant_dynamic-slice_fusion.9
  199.5 2.6 constant_dynamic-slice_fusion.9
  234.9 4.0 %collective-permute-start.9 = (f32[2,32,128]{1,0,2:T(2,128)S(1)}, f32[2,32,128]{1,0,2:T(2,128)S(1)}, u32[]{:S(2)}, u32[]{:S(2)}) collective-permute-start(f32[2,32,128]{1,0,2:T(2,128)S(1)} %get-tuple-element.119), channel_id=1, source_target_pairs={{0,16},{16,32},{32,48},{48,64},{64,80},{80,96},{96,112},{112,128},... | collective-permute-start | bytes 98312 | tf_op jit(solution)/shard_map/ppermute | solution.py:15
  241.2 2.7 fusion.47
  243.9 2.7 copy.94
  246.6 7.8 %collective-permute-start.11 = (f32[28,2,128]{2,0,1:T(8,128)S(1)}, f32[28,2,128]{2,0,1:T(8,128)S(1)}, u32[]{:S(2)}, u32[]{:S(2)}) collective-permute-start(f32[28,2,128]{2,0,1:T(8,128)S(1)} %copy.94), channel_id=1, source_target_pairs={{0,4},{4,8},{8,12},{1,5},{5,9},{9,13},{2,6},{6,10},{10,14},{3,7},{... | collective-permute-start | bytes 86024 | tf_op jit(solution)/shard_map/ppermute | solution.py:15
  254.4 2.7 copy.95
  258.9 2.8 copy.96
  261.8 4.4 %collective-permute-done.12 = f32[28,2,128]{2,0,1:T(8,128)S(1)} collective-permute-done((f32[28,2,128]{2,0,1:T(8,128)S(1)}, f32[28,2,128]{2,0,1:T(8,128)S(1)}, u32[]{:S(2)}, u32[]{:S(2)}) %collective-permute-start.12) | collective-permute-done | bytes 28704 | tf_op jit(solution)/shard_map/ppermute | solution.py:18
  266.1 2.9 copy.97
  269.9 3.1 collective-permute-start.13
  274.4 105.0 %psum.7 = f32[]{:T(128)} all-reduce(f32[]{:T(128)} %get-tuple-element.99), channel_id=1, replica_groups=mesh['gx'=32,'gy'=4,'gz'=4] {'gx','gy','gz'}, use_global_device_ids=true, to_apply=%region_4.5 | all-reduce | flops 1 | bytes 8 | tf_op jit(solution)/shard_map/psum | solution.py:121
  380.0 3.6 pad_maximum_fusion.2
  (344 shorter events, 128.7 us)
Async XLA Ops:
  0.6 11.0 %copy-start.3 = (f32[24,32,128]{2,1,0:T(8,128)S(1)}, f32[24,32,128]{2,1,0:T(8,128)}, u32[]{:S(2)}) copy-start(f32[24,32,128]{2,1,0:T(8,128)} %param.6) | copy-start | bytes 1179652
  1.5 29.3 %collective-permute-start.6 = (f32[3,32,128]{2,1,0:T(8,128)S(1)}, f32[3,32,128]{2,1,0:T(8,128)S(1)}, u32[]{:S(2)}, u32[]{:S(2)}) collective-permute-start(f32[3,32,128]{2,1,0:T(8,128)S(1)} %slice_bitcast_fusion.1), channel_id=1, source_target_pairs={{16,0},{32,16},{48,32},{64,48},{80,64},{96,80},{112,96},{128,112},... | collective-permute-start | bytes 147464 | tf_op jit(solution)/shard_map/ppermute | solution.py:26
  3.6 8.0 %collective-permute-start = (f32[2,32,128]{2,1,0:T(8,128)S(1)}, f32[2,32,128]{2,1,0:T(8,128)S(1)}, u32[]{:S(2)}, u32[]{:S(2)}) collective-permute-start(f32[2,32,128]{2,1,0:T(8,128)S(1)} %get-tuple-element.124), channel_id=1, source_target_pairs={{0,16},{16,32},{32,48},{48,64},{64,80},{80,96},{96,112},{112,128},... | collective-permute-start | bytes 98312 | tf_op jit(solution)/shard_map/ppermute | solution.py:15
  8.2 4.7 %collective-permute-start.1 = (f32[2,32,128]{2,1,0:T(8,128)S(1)}, f32[2,32,128]{2,1,0:T(8,128)S(1)}, u32[]{:S(2)}, u32[]{:S(2)}) collective-permute-start(f32[2,32,128]{2,1,0:T(8,128)S(1)} %get-tuple-element.123), channel_id=1, source_target_pairs={{16,0},{32,16},{48,32},{64,48},{80,64},{96,80},{112,96},{128,112},... | collective-permute-start | bytes 98312 | tf_op jit(solution)/shard_map/ppermute | solution.py:18
  12.9 20.5 %collective-permute-start.2 = (f32[28,2,128]{2,0,1:T(8,128)S(1)}, f32[28,2,128]{2,0,1:T(8,128)S(1)}, u32[]{:S(2)}, u32[]{:S(2)}) collective-permute-start(f32[28,2,128]{2,0,1:T(8,128)S(1)} %copy.103), channel_id=1, source_target_pairs={{0,4},{4,8},{8,12},{1,5},{5,9},{9,13},{2,6},{6,10},{10,14},{3,7},{... | collective-permute-start | bytes 86024 | tf_op jit(solution)/shard_map/ppermute | solution.py:15
  26.0 10.3 %collective-permute-start.3 = (f32[28,2,128]{2,0,1:T(8,128)S(1)}, f32[28,2,128]{2,0,1:T(8,128)S(1)}, u32[]{:S(2)}, u32[]{:S(2)}) collective-permute-start(f32[28,2,128]{2,0,1:T(8,128)S(1)} %copy.104), channel_id=1, source_target_pairs={{4,0},{8,4},{12,8},{5,1},{9,5},{13,9},{6,2},{10,6},{14,10},{7,3},{... | collective-permute-start | bytes 86024 | tf_op jit(solution)/shard_map/ppermute | solution.py:18
  39.2 9.2 %copy-start = (f32[28,32,128]{1,0,2:T(8,128)S(1)}, f32[28,32,128]{1,0,2:T(8,128)}, u32[]{:S(2)}) copy-start(f32[28,32,128]{1,0,2:T(8,128)} %copy.84) | copy-start | bytes 1376260
  39.2 9.2 %copy-start.1 = (f32[28,2,128]{1,0,2:T(8,128)S(1)}, f32[28,2,128]{1,0,2:T(8,128)}, u32[]{:S(2)}) copy-start(f32[28,2,128]{1,0,2:T(8,128)} %copy.83) | copy-start | bytes 86020
  39.2 9.2 %copy-start.2 = (f32[28,2,128]{1,0,2:T(8,128)S(1)}, f32[28,2,128]{1,0,2:T(8,128)}, u32[]{:S(2)}) copy-start(f32[28,2,128]{1,0,2:T(8,128)} %copy.85) | copy-start | bytes 86020
  40.3 6.6 %collective-permute-start.4 = (f32[28,36,2]{1,0,2:T(8,128)S(1)}, f32[28,36,2]{1,0,2:T(8,128)S(1)}, u32[]{:S(2)}, u32[]{:S(2)}) collective-permute-start(f32[28,36,2]{1,0,2:T(8,128)S(1)} %get-tuple-element.113), channel_id=1, source_target_pairs={{0,1},{1,2},{2,3},{4,5},{5,6},{6,7},{8,9},{9,10},{10,11},{12,13},{... | collective-permute-start | bytes 24200 | tf_op jit(solution)/shard_map/ppermute | solution.py:15
  43.7 4.7 %collective-permute-start.5 = (f32[28,36,2]{1,0,2:T(8,128)S(1)}, f32[28,36,2]{1,0,2:T(8,128)S(1)}, u32[]{:S(2)}, u32[]{:S(2)}) collective-permute-start(f32[28,36,2]{1,0,2:T(8,128)S(1)} %get-tuple-element.114), channel_id=1, source_target_pairs={{1,0},{2,1},{3,2},{5,4},{6,5},{7,6},{9,8},{10,9},{11,10},{13,12},{... | collective-permute-start | bytes 24200 | tf_op jit(solution)/shard_map/ppermute | solution.py:18
  45.0 9.6 %collective-permute-start.7 = (f32[3,25,128]{2,1,0:T(8,128)S(1)}, f32[3,25,128]{2,1,0:T(8,128)S(1)}, u32[]{:S(2)}, u32[]{:S(2)}) collective-permute-start(f32[3,25,128]{2,1,0:T(8,128)S(1)} %slice_bitcast_fusion), channel_id=1, source_target_pairs={{4,0},{8,4},{12,8},{5,1},{9,5},{13,9},{6,2},{10,6},{14,10},{7,3},{... | collective-permute-start | bytes 115208 | tf_op jit(solution)/shard_map/ppermute | solution.py:26
  58.3 5.7 %collective-permute-start.8 = (f32[3,25,33]{2,1,0:T(8,128)S(1)}, f32[3,25,33]{2,1,0:T(8,128)S(1)}, u32[]{:S(2)}, u32[]{:S(2)}) collective-permute-start(f32[3,25,33]{2,1,0:T(8,128)S(1)} %bitcast.81), channel_id=1, source_target_pairs={{1,0},{2,1},{3,2},{5,4},{6,5},{7,6},{9,8},{10,9},{11,10},{13,12},{... | collective-permute-start | bytes 29708 | tf_op jit(solution)/shard_map/ppermute | solution.py:26
  66.6 4.2 %copy-start.4 = (f32[24,24]{1,0:T(8,128)S(1)}, f32[24,24]{1,0:T(8,128)}, u32[]{:S(2)}) copy-start(f32[24,24]{1,0:T(8,128)} %constant.13.clone..sunk.2) | copy-start | bytes 6916
  233.6 5.7 %collective-permute-start.10 = (f32[2,32,128]{1,0,2:T(2,128)S(1)}, f32[2,32,128]{1,0,2:T(2,128)S(1)}, u32[]{:S(2)}, u32[]{:S(2)}) collective-permute-start(f32[2,32,128]{1,0,2:T(2,128)S(1)} %get-tuple-element.120), channel_id=1, source_target_pairs={{16,0},{32,16},{48,32},{64,48},{80,64},{96,80},{112,96},{128,112},... | collective-permute-start | bytes 98312 | tf_op jit(solution)/shard_map/ppermute | solution.py:18
  234.9 5.9 %collective-permute-start.9 = (f32[2,32,128]{1,0,2:T(2,128)S(1)}, f32[2,32,128]{1,0,2:T(2,128)S(1)}, u32[]{:S(2)}, u32[]{:S(2)}) collective-permute-start(f32[2,32,128]{1,0,2:T(2,128)S(1)} %get-tuple-element.119), channel_id=1, source_target_pairs={{0,16},{16,32},{32,48},{48,64},{64,80},{80,96},{96,112},{112,128},... | collective-permute-start | bytes 98312 | tf_op jit(solution)/shard_map/ppermute | solution.py:15
  246.6 12.4 %collective-permute-start.11 = (f32[28,2,128]{2,0,1:T(8,128)S(1)}, f32[28,2,128]{2,0,1:T(8,128)S(1)}, u32[]{:S(2)}, u32[]{:S(2)}) collective-permute-start(f32[28,2,128]{2,0,1:T(8,128)S(1)} %copy.94), channel_id=1, source_target_pairs={{0,4},{4,8},{8,12},{1,5},{5,9},{9,13},{2,6},{6,10},{10,14},{3,7},{... | collective-permute-start | bytes 86024 | tf_op jit(solution)/shard_map/ppermute | solution.py:15
  257.0 9.1 %collective-permute-start.12 = (f32[28,2,128]{2,0,1:T(8,128)S(1)}, f32[28,2,128]{2,0,1:T(8,128)S(1)}, u32[]{:S(2)}, u32[]{:S(2)}) collective-permute-start(f32[28,2,128]{2,0,1:T(8,128)S(1)} %copy.95), channel_id=1, source_target_pairs={{4,0},{8,4},{12,8},{5,1},{9,5},{13,9},{6,2},{10,6},{14,10},{7,3},{... | collective-permute-start | bytes 86024 | tf_op jit(solution)/shard_map/ppermute | solution.py:18
  269.9 110.1 %collective-permute-start.13 = (f32[28,36,2]{1,0,2:T(8,128)S(1)}, f32[28,36,2]{1,0,2:T(8,128)S(1)}, u32[]{:S(2)}, u32[]{:S(2)}) collective-permute-start(f32[28,36,2]{1,0,2:T(8,128)S(1)} %get-tuple-element.115), channel_id=1, source_target_pairs={{0,1},{1,2},{2,3},{4,5},{5,6},{6,7},{8,9},{9,10},{10,11},{12,13},{... | collective-permute-start | bytes 24200 | tf_op jit(solution)/shard_map/ppermute | solution.py:15
  273.1 107.0 %collective-permute-start.14 = (f32[28,36,2]{1,0,2:T(8,128)S(1)}, f32[28,36,2]{1,0,2:T(8,128)S(1)}, u32[]{:S(2)}, u32[]{:S(2)}) collective-permute-start(f32[28,36,2]{1,0,2:T(8,128)S(1)} %get-tuple-element.116), channel_id=1, source_target_pairs={{1,0},{2,1},{3,2},{5,4},{6,5},{7,6},{9,8},{10,9},{11,10},{13,12},{... | collective-permute-start | bytes 24200 | tf_op jit(solution)/shard_map/ppermute | solution.py:18
where the time goes:
time: 391 us; the launch traced here: 389 us
  local copies, waits for them, and re-layouts  128 us (33%)
  blocking collectives  105 us (27%)
  starting transfers between devices  49.6 us (13%)
  loops' own time  47.1 us (12%)
  other arithmetic  21.9 us (6%)
  matrix products  20.4 us (5%)
  waiting for transfers between devices  14 us (4%)
    psum x1, blocking collectives, shards(): total = lax.psum(local_total, ('gx', 'gy', 'gz'))  105 us
    slice x24, local copies, waits for them, and re-layouts, slab(): corners.append(source[:, corner // 4, shift_y:shift_y + rows, :])  61.5 us
    another operation x1, loops' own time, element_energy(): return lax.map(slab, jnp.arange(low.shape[1] - 1, dtype=jnp.int32))  47.1 us
    ppermute x6, starting transfers between devices, extended_2(): lax.ppermute(lax.slice_in_dim(block, block.shape[dim] - width, None, axis...  36 us
    dot_general x24, matrix products, slab(): image = jnp.dot(stiffness, vector, precision=lax.Precision.HIGHEST)  20.4 us
    dynamic_update_slice x24, local copies, waits for them, and re-layouts, element_energy(): return lax.map(slab, jnp.arange(low.shape[1] - 1, dtype=jnp.int32))  14.7 us
    dynamic_slice x24, local copies, waits for them, and re-layouts, element_energy(): return lax.map(slab, jnp.arange(low.shape[1] - 1, dtype=jnp.int32))  14.3 us
    ppermute x6, starting transfers between devices, extended_2(): lax.ppermute(lax.slice_in_dim(block, 0, width, axis=dim), axis, backward)  9 us
  transfers between devices with their start and end apart: 15, of which 7 were waited for; matrix products, arithmetic and copies ran while one was open for 6% of the time, Pallas kernels for 0%

commit v1 on v0

v1 whole, which is shorter than its diff:
```python
import functools
import itertools

import jax
import jax.numpy as jnp
from jax import lax
from jax.experimental import pallas as pl
from jax.experimental.pallas import tpu as pltpu
from jax.sharding import PartitionSpec as P

MESH = pl.DeviceIdType.MESH
F32 = jnp.float32
NX, NY, NZ = 24, 32, 128
ROWS = NX * NY
GROUPS = ROWS // 128
YPAD = 48
NODE_PAD = 40
LAME = 0.3 / (1.3 * 0.4)
SHEAR = 1.0 / 2.6

DIRECTIONS = [d for d in itertools.product((-1, 0, 1), repeat=3) if any(d)]
LOWER = [d for d in DIRECTIONS if max(d) <= 0]


def slot(direction):
    return (direction[0] + 1) * 9 + (direction[1] + 1) * 3 + direction[2] + 1


def lower_slot(direction):
    return -(direction[0] * 4 + direction[1] * 2 + direction[2])


def iota(shape, axis):
    return lax.broadcasted_iota(jnp.int32, shape, axis)


def hat_lanes(v):
    lane = iota(v.shape, v.ndim - 1)
    axis = v.ndim - 1

    def moved(step):
        rolled = pltpu.roll(v, step % NZ, axis)
        return jnp.where(lane >= step if step > 0 else lane < NZ + step, rolled, 0.0)

    return 3.0 * v + 2.0 * (moved(1) + moved(-1)) + (moved(2) + moved(-2))


def across(v, axis, size, step, direction):
    place = iota(v.shape, axis) // step
    count = size // step
    if direction > 0:
        two, one = pltpu.roll(v, 2 * step, axis), pltpu.roll(v, step, axis)
        return jnp.where(place == 0, two + 2.0 * one, jnp.where(place == 1, two, 0.0))
    two, one = pltpu.roll(v, size - 2 * step, axis), pltpu.roll(v, size - step, axis)
    return jnp.where(place == count - 1, two + 2.0 * one, jnp.where(place == count - 2, two, 0.0))


def kernel(sizes, density, displacement, out, total_out, *scratch):
    (field, g, b4, h, acc, rows, corner, nodes, hz, sd, last, energy,
     xs, ys, xys, zs, xzs, yzs, xyzs, xr, yr, xyr, zr, xzr, yzr, xyzr,
     dys, dxys, dzs, dxzs, dyzs, dxyzs, dzr, dxzr, dyzr, dxyzr, m6,
     part, part_in, send_sem, recv_sem, dsend_sem, drecv_sem, load_sem, psend_sem, precv_sem) = scratch
    size_x, size_y, size_z, ring_y = sizes
    gx, gy, gz = (lax.axis_index(a) for a in ("gx", "gy", "gz"))

    def inside(direction):
        ok = []
        for place, step, count in zip((gx, gy, gz), direction, (size_x, size_y, size_z)):
            if step > 0:
                ok.append(place < count - 1)
            elif step < 0:
                ok.append(place > 0)
        return functools.reduce(jnp.logical_and, ok)

    def device(direction):
        return (gx + direction[0], gy + direction[1], gz + direction[2])

    layers_z = size_x // ring_y
    my_y, my_z = lax.rem(gx, ring_y), gx // ring_y + layers_z * (gy // 2)
    my_core = lax.rem(gy, 2)
    count_z = layers_z * (size_y // 2)

    def partner_zc(dz, dc):
        z, c = lax.rem(my_z + dz, count_z), lax.rem(my_core + dc, 2)
        return (lax.rem(z, layers_z) * ring_y + my_y, (z // layers_z) * 2 + c, gz)

    def partner_xy(dx, dy):
        x, y = lax.rem(gz + dx, size_z), lax.rem(my_y + dy, ring_y)
        return ((gx // ring_y) * ring_y + y, gy, x)

    def far_first(counts):
        offs = [o for o in itertools.product(*[range(c) for c in counts]) if any(o)]
        return sorted(offs, key=lambda o: -sum(min(s, c - s) for s, c in zip(o, counts)))

    stages = [
        (partner_zc, far_first((count_z, 2)), my_z * 2 + my_core),
        (partner_xy, far_first((size_z, ring_y)), gz * ring_y + my_y),
    ]

    load_density = pltpu.make_async_copy(density, field.at[pl.ds(2 * NY, ROWS)], load_sem.at[0])
    load_nodes = pltpu.make_async_copy(displacement, nodes.at[:, pl.ds(0, ROWS)], load_sem.at[1])
    load_density.start()
    load_nodes.start()

    zero_row = jnp.zeros((8, NZ), F32)

    def zero(ref):
        ref[...] = jnp.zeros(ref.shape, F32)

    received = {}
    for d in DIRECTIONS:
        sx, sy, sz = ((s + 1) // 2 for s in d)
        kind = tuple(bool(s) for s in d)
        received[d] = {
            (True, False, False): lambda p: (xs.at[p, sx], xr.at[p, sx]),
            (False, True, False): lambda p: (ys.at[p, sy], yr.at[p, sy]),
            (True, True, False): lambda p: (xys.at[p, sx, sy], xyr.at[p, sx, sy]),
            (False, False, True): lambda p: (zs.at[p, sz], zr.at[p, sz]),
            (True, False, True): lambda p: (xzs.at[p, sx, sz], xzr.at[p, sx, sz]),
            (False, True, True): lambda p: (yzs.at[p, sy, sz], yzr.at[p, sy, sz]),
            (True, True, True): lambda p: (xyzs.at[p, sx, sy, sz], xyzr.at[p, sx, sy, sz]),
        }[kind]
        received[d] = [received[d](p) for p in range(2)]
    lower = {
        (-1, 0, 0): (nodes.at[:, pl.ds(0, NY)], nodes.at[:, pl.ds(ROWS, NY)]),
        (0, -1, 0): (dys, nodes.at[:, pl.ds(ROWS + NY, NX)]),
        (-1, -1, 0): (dxys, nodes.at[:, pl.ds(ROWS + NY + NX, 8)]),
        (0, 0, -1): (dzs, dzr),
        (-1, 0, -1): (dxzs, dxzr),
        (0, -1, -1): (dyzs, dyzr),
        (-1, -1, -1): (dxyzs, dxyzr),
    }

    for d in DIRECTIONS:
        @pl.when(jnp.logical_not(inside(tuple(-s for s in d))))
        def _(d=d):
            for p in range(2):
                zero(received[d][p][1])
            if d in lower:
                zero(lower[d][1])

    barrier = pltpu.get_barrier_semaphore()
    waits = 0
    for d in DIRECTIONS:
        @pl.when(inside(d))
        def _(d=d):
            pl.semaphore_signal(barrier, inc=1, device_id=device(d), device_id_type=MESH)
        waits = waits + inside(d).astype(jnp.int32)
    for partner, offsets, _ in stages:
        for o in offsets:
            pl.semaphore_signal(barrier, inc=1, device_id=partner(*o), device_id_type=MESH)
        waits = waits + len(offsets)

    def remote(source, target, send, recv, to):
        return pltpu.make_async_remote_copy(
            src_ref=source, dst_ref=target, send_sem=send, recv_sem=recv, device_id=to, device_id_type=MESH)

    def filter_copy(p, d):
        source, target = received[d][p]
        return remote(source, target, send_sem.at[p, slot(d)], recv_sem.at[p, slot(d)], device(d))

    def lower_copy(d):
        source, target = lower[d]
        return remote(source, target, dsend_sem.at[lower_slot(d)], drecv_sem.at[lower_slot(d)], device(d))

    for margin in (0, NY, (NX + 2) * NY, (NX + 3) * NY):
        field[pl.ds(margin, NY), :] = jnp.zeros((NY, NZ), F32)

    def clear(i, _):
        base = pl.multiple_of(i * YPAD, 16)
        g[pl.ds(base, 8), :] = zero_row
        g[pl.ds(base + 40, 8), :] = zero_row
        return 0

    lax.fori_loop(0, NX, clear, 0)
    for i in range(4):
        b4[pl.ds(i * YPAD, 8), :] = zero_row
        b4[pl.ds(i * YPAD + 40, 8), :] = zero_row
    zero(rows)
    zero(corner)
    zero(m6)

    def hat_rows(ref, base):
        at = [ref[pl.ds(base + 6 + k, NY), :] for k in range(5)]
        return 3.0 * at[2] + 2.0 * (at[1] + at[3]) + (at[0] + at[4])

    def local_filter(p):
        for n, layer in enumerate((0, 1, NX - 2, NX - 1)):
            b4[pl.ds(n * YPAD + 8, NY), :] = field[pl.ds((layer + 2) * NY, NY), :]
        faces = [hat_rows(b4, n * YPAD) for n in range(4)]
        for n in range(4):
            xs[p, n // 2, pl.ds((n % 2) * NY, NY), :] = hat_lanes(faces[n])
        turned = jnp.concatenate(faces, 0).T
        for sz, part_z in enumerate((turned[0:8], turned[120:128])):
            for sx in range(2):
                xzs[p, sx, sz] = across(part_z, 1, 128, 32, 2 * sx - 1)

        def x_pass(i, _):
            at = [field[pl.ds(pl.multiple_of((i + k) * NY, NY), NY), :] for k in range(5)]
            g[pl.ds(pl.multiple_of(i * YPAD, 16) + 8, NY), :] = 3.0 * at[2] + 2.0 * (at[1] + at[3]) + (at[0] + at[4])
            return 0

        lax.fori_loop(0, NX, x_pass, 0)

        for n, row in enumerate((0, 1, NY - 2, NY - 1)):
            edge = g[pl.ds(8 + row, NX, stride=YPAD), :]
            rows[pl.ds(n * 32, NX), :] = edge
            ys[p, n // 2, n % 2] = hat_lanes(edge)
            raw = field[pl.ds(2 * NY + row, NX, stride=NY), :]
            up, down = across(raw[NX - 8:], 0, 8, 1, 1), across(raw[:8], 0, 8, 1, -1)
            corner[pl.ds(n * 32, 8), :] = up
            corner[pl.ds(n * 32 + NX - 8, 8), :] = down
            xys[p, 1, n // 2, n % 2] = hat_lanes(up)
            xys[p, 0, n // 2, n % 2] = hat_lanes(down)
        turned = rows[...].T
        for sz, part_z in enumerate((turned[0:8], turned[120:128])):
            for sy in range(2):
                yzs[p, sy, sz] = across(part_z, 1, 128, 32, 2 * sy - 1)
        turned = corner[...].T
        lane = lax.rem(iota((8, 128), 1), 32)
        for sz, part_z in enumerate((turned[0:8], turned[120:128])):
            for sy in range(2):
                both = across(part_z, 1, 128, 32, 2 * sy - 1)
                xyzs[p, 1, sy, sz] = jnp.where(lane < 8, both, 0.0)
                xyzs[p, 0, sy, sz] = jnp.where(lane < 8, 0.0, both)

        def y_pass(i, _):
            v = hat_rows(g, pl.multiple_of(i * YPAD, 16))
            h[pl.ds(pl.multiple_of(i * NY, NY), NY), :] = v
            acc[pl.ds(pl.multiple_of(i * NY, NY), NY), :] = hat_lanes(v)
            return 0

        lax.fori_loop(0, NX, y_pass, 0)
        for k in range(GROUPS):
            turned = h[pl.ds(k * 128, 128), :].T
            zs[p, 0, :, pl.ds(k * 128, 128)] = turned[0:8]
            zs[p, 1, :, pl.ds(k * 128, 128)] = turned[120:128]

    def send_filter(p):
        for d in DIRECTIONS:
            @pl.when(inside(d))
            def _(d=d):
                filter_copy(p, d).start()

    def add_received(p):
        for d in DIRECTIONS:
            @pl.when(inside(tuple(-s for s in d)))
            def _(d=d):
                filter_copy(p, d).wait_recv()
        def add(layer, v):
            acc[pl.ds(layer * NY, NY), :] = acc[pl.ds(layer * NY, NY), :] + v

        first, second = xr[p, 1, pl.ds(0, NY), :], xr[p, 1, pl.ds(NY, NY), :]
        add(0, first + 2.0 * second)
        add(1, second)
        first, second = xr[p, 0, pl.ds(0, NY), :], xr[p, 0, pl.ds(NY, NY), :]
        add(NX - 2, first)
        add(NX - 1, 2.0 * first + second)
        low = sum([yzr[p, sy, 1] for sy in range(2)] + [xyzr[p, sx, sy, 1] for sx in range(2) for sy in range(2)])
        high = sum([yzr[p, sy, 0] for sy in range(2)] + [xyzr[p, sx, sy, 0] for sx in range(2) for sy in range(2)])
        middle = jnp.zeros((112, 128), F32)
        turned = jnp.concatenate([across(low, 0, 8, 1, 1), middle, across(high, 0, 8, 1, -1)], 0).T
        at = {}
        for sy in range(2):
            for n in range(2):
                center = yr[p, sy, n]
                at[sy, n] = jnp.concatenate(
                    [center[:8] + xyr[p, 1, sy, n], center[8:16], center[16:] + xyr[p, 0, sy, n]], 0)
        for n, (row, v) in enumerate((
                (0, at[1, 0] + 2.0 * at[1, 1]), (1, at[1, 1]), (NY - 2, at[0, 0]), (NY - 1, 2.0 * at[0, 0] + at[0, 1]))):
            place = pl.ds(row, NX, stride=NY)
            acc[place, :] = acc[place, :] + v + turned[n * 32:n * 32 + NX]
        for k in range(GROUPS):
            low, high = zr[p, 1, :, pl.ds(k * 128, 128)], zr[p, 0, :, pl.ds(k * 128, 128)]
            if k == 0:
                low, high = low + xzr[p, 1, 1], high + xzr[p, 1, 0]
            if k == GROUPS - 1:
                low, high = low + xzr[p, 0, 1], high + xzr[p, 0, 0]
            turned = jnp.concatenate([across(low, 0, 8, 1, 1), middle, across(high, 0, 8, 1, -1)], 0).T
            acc[pl.ds(k * 128, 128), :] = acc[pl.ds(k * 128, 128), :] + turned

    load_density.wait()
    local_filter(0)
    load_nodes.wait()

    def first_columns(v):
        lane = iota(v[0].shape, 1)
        return jnp.where(lane == 0, v[0], jnp.where(
            lane == 1, pltpu.roll(v[1], 1, 1), jnp.where(lane == 2, pltpu.roll(v[2], 2, 1), 0.0)))

    for m in range(3):
        dys[m] = nodes[m, pl.ds(0, NX, stride=NY), :]
        dxys[m] = dys[m, pl.ds(0, 8), :]
    for k in range(GROUPS):
        columns = first_columns([nodes[m, pl.ds(k * 128, 128), :] for m in range(3)])
        dzs[:, pl.ds(k * 128, 128)] = columns.T[0:8]
        if k == 0:
            m6[pl.ds(0, NY), :] = columns[:NY]
    m6[pl.ds(NY, NX), :] = first_columns([dys[m] for m in range(3)])
    turned = m6[...].T[0:8]
    lane8 = iota((8, 128), 1)
    dxzs[...] = jnp.where(lane8 < NY, turned, 0.0)
    dyzs[...] = jnp.where(jnp.logical_and(lane8 >= NY, lane8 < NY + NX), turned, 0.0)
    dxyzs[...] = jnp.where(lane8 == NY + NX, pltpu.roll(turned, NY + NX, 1), 0.0)

    pl.semaphore_wait(barrier, waits)
    for d in LOWER:
        @pl.when(inside(d))
        def _(d=d):
            lower_copy(d).start()
    send_filter(0)

    for d in LOWER:
        @pl.when(inside(tuple(-s for s in d)))
        def _(d=d):
            lower_copy(d).wait_recv()
    rest = jnp.zeros((120, 128), F32)
    for k in range(GROUPS + 1):
        if k < GROUPS:
            packed = dzr[:, pl.ds(k * 128, 128)]
        else:
            packed = dxzr[...] + dyzr[...] + dxyzr[...]
        turned = jnp.concatenate([packed, rest], 0).T
        if k < GROUPS:
            hz[pl.ds(k * 128, 128), :] = turned
        else:
            hz[pl.ds(k * 128, 64), :] = turned[:64]

    def z_pass(base):
        halo = hz[pl.ds(base, NY), :]
        lane = iota(halo.shape, 1)
        out = []
        for m in range(3):
            u = nodes[m, pl.ds(base, NY), :]
            t = halo if m == 0 else pltpu.roll(halo, NZ - m, 1)
            up = pltpu.roll(jnp.where(lane == 0, t, u), NZ - 1, 1)
            out += [u + up, up - u]
        return out

    for k, v in enumerate(z_pass(ROWS + NY)):
        last[k] = v

    def z_layer(i, _):
        base = pl.multiple_of(i * NODE_PAD, 8)
        for k, v in enumerate(z_pass(pl.multiple_of(i * NY, NY))):
            sd[k, pl.ds(base, NY), :] = v
            sd[k, pl.ds(base + NY, 1), :] = last[k, pl.ds(i, 1), :]
        return 0

    lax.fori_loop(0, NX + 1, z_layer, 0)

    def yz_terms(i, t):
        base = pl.multiple_of(i * NODE_PAD, 8) + 8 * t
        out = []
        for k in range(6):
            here, above = sd[k, pl.ds(base, 8), :], sd[k, pl.ds(base + 1, 8), :]
            out += [here + above, above - here]
        return out

    square = lambda v: v * v

    for t in range(NY // 8):
        def element(i, before, t=t):
            now = yz_terms(i, t)
            w = []
            for m in range(3):
                (a0, a1, a2, a3), (b0, b1, b2, b3) = now[4 * m:4 * m + 4], before[4 * m:4 * m + 4]
                w.append({100: a0 - b0, 110: a1 - b1, 101: a2 - b2, 111: a3 - b3,
                          10: a1 + b1, 1: a2 + b2, 11: a3 + b3})
            u, v, z = w
            total = (LAME / 16) * square(u[100] + v[10] + z[1])
            total += (LAME / 48) * (square(v[110] + z[101]) + square(u[110] + z[11]) + square(u[101] + v[11]))
            total += (SHEAR / 8) * (square(u[100]) + square(v[10]) + square(z[1]))
            total += (SHEAR / 16) * (
                (square(u[110]) + square(u[101]) + square(v[110])) + (square(v[11]) + square(z[101]) + square(z[11]))
                + (square(u[10] + v[100]) + square(v[1] + z[10]) + square(u[1] + z[100])))
            total += (SHEAR / 48) * (square(u[11] + v[101]) + square(v[101] + z[110]) + square(u[11] + z[110]))
            total += ((LAME + 4 * SHEAR) / 144) * (square(u[111]) + square(v[111]) + square(z[111]))
            energy[pl.ds(pl.multiple_of((i - 1) * NY, NY) + 8 * t, 8), :] = total
            return tuple(now)

        lax.fori_loop(1, NX + 1, element, tuple(yz_terms(0, t)))

    add_received(0)

    def inverse_cover(index, extent):
        end = extent - 1
        return jnp.where(jnp.logical_or(index == 0, index == end), 1.0 / 6.0, jnp.where(
            jnp.logical_or(index == 1, index == end - 1), 1.0 / 8.0, 1.0 / 9.0)).astype(F32)

    inverse_yz = inverse_cover(iota((NY, NZ), 0) + gy * NY, NY * size_y) * inverse_cover(
        iota((NY, NZ), 1) + gz * NZ, NZ * size_z)

    def weigh(i, total):
        base = pl.multiple_of(i * NY, NY)
        inverse = inverse_yz * inverse_cover(gx * NX + i, NX * size_x)
        physical = acc[pl.ds(base, NY), :] * inverse
        product = physical * physical * energy[pl.ds(base, NY), :]
        field[pl.ds(base + 2 * NY, NY), :] = -3.0 * product * inverse
        return total + physical * product

    total = lax.fori_loop(0, NX, weigh, jnp.zeros((NY, NZ), F32))
    total = jnp.sum(total, axis=0, keepdims=True)

    def send_total(s, value):
        partner, offsets, mine = stages[s]
        part[s] = value
        part_in[s, mine] = value
        for o in offsets:
            remote(part.at[s], part_in.at[s, mine], psend_sem.at[s], precv_sem.at[s], partner(*o)).start()

    def total_wait(s, sem):
        n = len(stages[s][1])
        whole = part_in.at[s, pl.ds(0, n)]
        pltpu.make_async_copy(whole, whole, sem.at[s]).wait()

    def receive_total(s):
        total_wait(s, precv_sem)
        return jnp.sum(part_in[s, 0:len(stages[s][1]) + 1], axis=0)

    send_total(0, total)
    local_filter(1)
    send_filter(1)
    send_total(1, receive_total(0))
    add_received(1)
    out[...] = acc[...]
    total = receive_total(1)
    total_out[...] = jnp.broadcast_to(jnp.sum(total, axis=1, keepdims=True), (8, 128))

    for d in DIRECTIONS:
        @pl.when(inside(d))
        def _(d=d):
            for p in range(2):
                filter_copy(p, d).wait_send()
            if d in lower:
                lower_copy(d).wait_send()
    for s in range(2):
        total_wait(s, psend_sem)


def exchange(mesh, density, displacement):
    sizes = (mesh.shape["gx"], mesh.shape["gy"], mesh.shape["gz"], min(8, mesh.shape["gx"]))
    vmem = lambda *shape: pltpu.VMEM(shape, F32)
    partners = max(sizes[0] // sizes[3] * sizes[1], sizes[3] * sizes[2])
    scratch = [
        vmem((NX + 4) * NY, NZ), vmem(NX * YPAD, NZ), vmem(4 * YPAD, NZ), vmem(ROWS, NZ), vmem(ROWS, NZ),
        vmem(128, NZ), vmem(128, NZ), vmem(3, ROWS + 2 * NY, NZ), vmem(ROWS + 2 * NY, NZ),
        vmem(6, (NX + 1) * NODE_PAD, NZ), vmem(6, NY, NZ), vmem(ROWS, NZ)]
    filters = [vmem(2, 2, 2 * NY, NZ), vmem(2, 2, 2, NX, NZ), vmem(2, 2, 2, 2, 8, NZ), vmem(2, 2, 8, ROWS),
               vmem(2, 2, 2, 8, 128), vmem(2, 2, 2, 8, 128), vmem(2, 2, 2, 2, 8, 128)]
    scratch += filters + filters
    scratch += [vmem(3, NX, NZ), vmem(3, 8, NZ), vmem(8, ROWS), vmem(8, 128), vmem(8, 128), vmem(8, 128),
                vmem(8, ROWS), vmem(8, 128), vmem(8, 128), vmem(8, 128), vmem(128, 128)]
    scratch += [vmem(2, 1, 128), vmem(2, partners, 1, 128)]
    dma = pltpu.SemaphoreType.DMA
    scratch += [dma((2, 27)), dma((2, 27)), dma((8,)), dma((8,)), dma((2,)), dma((2,)), dma((2,))]
    return pl.pallas_call(
        functools.partial(kernel, sizes),
        out_shape=[jax.ShapeDtypeStruct((ROWS, NZ), F32), jax.ShapeDtypeStruct((8, 128), F32)],
        in_specs=[pl.BlockSpec(memory_space=pl.ANY)] * 2,
        out_specs=[pl.BlockSpec(memory_space=pltpu.VMEM)] * 2,
        scratch_shapes=scratch,
        compiler_params=pltpu.CompilerParams(
            collective_id=0, has_side_effects=True, vmem_limit_bytes=40 * 2**20),
        cost_estimate=pl.CostEstimate(flops=20_000_000, bytes_accessed=2_000_000, transcendentals=0),
    )(density, displacement)


def scale_kernel(elements, field, total, out, mean_out):
    mean = total[0:1, :] / elements
    out[...] = field[...] / mean
    mean_out[...] = mean[:, 0:1]


def solution(mesh):
    def shards(displacement, density):
        filtered, total = exchange(mesh, density.reshape(ROWS, NZ), displacement.reshape(3, ROWS, NZ))
        sensitivity, mean = pl.pallas_call(
            functools.partial(scale_kernel, float(ROWS * NZ * mesh.size)),
            out_shape=[jax.ShapeDtypeStruct((ROWS, NZ), F32), jax.ShapeDtypeStruct((1, 1), F32)],
        )(filtered, total)
        return sensitivity.reshape(NX, NY, NZ), mean.reshape(())

    return jax.shard_map(
        shards,
        mesh=mesh,
        in_specs=(P(None, "gx", "gy", "gz"), P("gx", "gy", "gz")),
        out_specs=(P("gx", "gy", "gz"), P()),
        check_vma=False,
    )
```

time: 391 us -> 45.8 us (0.12)
  local copies, waits for them, and re-layouts: 128 us -> 3.59 us
  blocking collectives: 105 us -> 0 us
  starting transfers between devices: 49.6 us -> 0 us
  loops' own time: 47.1 us -> 0 us
  Pallas kernels: 0 us -> 41.3 us
  other arithmetic: 21.9 us -> 0 us
  matrix products: 20.4 us -> 0 us
  waiting for transfers between devices: 14 us -> 0 us
    psum x1 -> x0, blocking collectives: 105 us -> none  [shards(): total = lax.psum(local_total, ('gx', 'gy', 'gz'))]
    slice x31 -> x0, local copies, waits for them, and re-layouts: 72.7 us -> none  [the longest x24 61.5 us: slab(): corners.append(source[:, corner // 4, shift_y:shift_y + rows, :])]
    ppermute x15 -> x0, starting transfers between devices: 49.6 us -> none  [the longest x6 36 us: extended_2(): lax.ppermute(lax.slice_in_dim(block, block.shape[dim] - width, None, axis...]
    another operation x1 -> x0, loops' own time: 47.1 us -> none  [element_energy(): return lax.map(slab, jnp.arange(low.shape[1] - 1, dtype=jnp.int32))]
    pallas_call x0 -> x2, Pallas kernels: none -> 41.3 us  [the longest x1 39.6 us: exchange(): pl.pallas_call(functools.partial(kernel, sizes), out_shape=[jax.ShapeDtyp...]
    dot_general x24 -> x0, matrix products: 20.4 us -> none  [slab(): image = jnp.dot(stiffness, vector, precision=lax.Precision.HIGHEST)]
    dynamic_update_slice x24 -> x0, local copies, waits for them, and re-layouts: 14.7 us -> none  [element_energy(): return lax.map(slab, jnp.arange(low.shape[1] - 1, dtype=jnp.int32))]
    dynamic_slice x24 -> x0, local copies, waits for them, and re-layouts: 14.3 us -> none  [element_energy(): return lax.map(slab, jnp.arange(low.shape[1] - 1, dtype=jnp.int32))]
  transfers between devices with their start and end apart: 15 -> 0, of which waited for: 7 -> 0; matrix products, arithmetic and copies ran while one was open for 6% -> 0% of each run, Pallas kernels for 0% -> 0%
where the time goes in v1:
time: 45.8 us; the launch traced here: 45.6 us
  Pallas kernels  41.3 us (90%)
  local copies, waits for them, and re-layouts  3.59 us (8%)
  between operations  0.66 us (1%)
    pallas_call x1, Pallas kernels, exchange(): pl.pallas_call(functools.partial(kernel, sizes), out_shape=[jax.ShapeDtyp...  39.6 us
    unnamed x8, local copies, waits for them, and re-layouts  3.59 us
    pallas_call x1, Pallas kernels, shards(): pl.pallas_call(functools.partial(scale_kernel, float(ROWS * NZ * mesh.siz...  1.78 us

profile of v1, /device:TPU:1, one launch (start us, length us, event | category | flops | bytes accessed | tf_op | source)
XLA Modules:
  0.0 45.6 jit_solution(5959310862209223777)
XLA Ops:
  0.6 0.0 copy-start
  0.6 1.3 %copy-done = f32[3,24,32,128]{3,2,1,0:T(8,128)S(1)} copy-done((f32[3,24,32,128]{3,2,1,0:T(8,128)S(1)}, f32[3,24,32,128]{3,2,1,0:T(8,128)}, u32[]{:S(2)}) %copy-start) | copy-done | bytes 1179672
  1.9 0.0 copy-start.2
  1.9 1.0 %copy-done.2 = f32[24,32,128]{2,1,0:T(8,128)S(1)} copy-done((f32[24,32,128]{2,1,0:T(8,128)S(1)}, f32[24,32,128]{2,1,0:T(8,128)}, u32[]{:S(2)}) %copy-start.2) | copy-done | bytes 393240
  2.9 39.6 %shard_map.41 = (f32[768,128]{1,0:T(8,128)S(1)}, f32[8,128]{1,0:T(8,128)S(1)}) custom-call(f32[768,128]{1,0:T(8,128)S(1)} %bitcast.5, f32[3,768,128]{2,1,0:T(8,128)S(1)} %bitcast.4), custom_call_target="tpu_custom_call" | custom-call | flops 20000000 | bytes 2000000 | tf_op jit(solution)/shard_map/pallas_call | solution.py:457
  42.5 0.0 copy-start.1
  42.5 0.7 %copy-done.1 = f32[768,128]{1,0:T(8,128)} copy-done((f32[768,128]{1,0:T(8,128)}, f32[768,128]{1,0:T(8,128)S(1)}, u32[]{:S(2)}) %copy-start.1) | copy-done | bytes 393240
  43.2 0.0 copy-start.3
  43.2 0.6 %copy-done.3 = f32[8,128]{1,0:T(8,128)} copy-done((f32[8,128]{1,0:T(8,128)}, f32[8,128]{1,0:T(8,128)S(1)}, u32[]{:S(2)}) %copy-start.3) | copy-done | bytes 4120
  43.8 1.8 %shard_map.42 = (f32[768,128]{1,0:T(8,128)}, f32[1,1]{1,0:T(1,128)}) custom-call(f32[768,128]{1,0:T(8,128)} %copy-done.1, f32[8,128]{1,0:T(8,128)} %copy-done.3), custom_call_target="tpu_custom_call" | custom-call | tf_op jit(solution)/shard_map/pallas_call | solution.py:478
Async XLA Ops:
  0.6 1.3 %copy-start = (f32[3,24,32,128]{3,2,1,0:T(8,128)S(1)}, f32[3,24,32,128]{3,2,1,0:T(8,128)}, u32[]{:S(2)}) copy-start(f32[3,24,32,128]{3,2,1,0:T(8,128)} %param.2) | copy-start | bytes 3538948
  1.9 1.0 %copy-start.2 = (f32[24,32,128]{2,1,0:T(8,128)S(1)}, f32[24,32,128]{2,1,0:T(8,128)}, u32[]{:S(2)}) copy-start(f32[24,32,128]{2,1,0:T(8,128)} %param.3) | copy-start | bytes 1179652
  42.5 0.7 %copy-start.1 = (f32[768,128]{1,0:T(8,128)}, f32[768,128]{1,0:T(8,128)S(1)}, u32[]{:S(2)}) copy-start(f32[768,128]{1,0:T(8,128)S(1)} %get-tuple-element.6.field) | copy-start | bytes 1179652
  43.2 0.6 %copy-start.3 = (f32[8,128]{1,0:T(8,128)}, f32[8,128]{1,0:T(8,128)S(1)}, u32[]{:S(2)}) copy-start(f32[8,128]{1,0:T(8,128)S(1)} %get-tuple-element.7.total) | copy-start | bytes 12292

commit v2 on v1

--- a/solution.py
+++ b/solution.py
@@ -15,10 +15,11 @@
 GROUPS = ROWS // 128
 YPAD = 48
 NODE_PAD = 40
+PARTS = 4
 LAME = 0.3 / (1.3 * 0.4)
 SHEAR = 1.0 / 2.6
 
-DIRECTIONS = [d for d in itertools.product((-1, 0, 1), repeat=3) if any(d)]
+DIRECTIONS = sorted((d for d in itertools.product((-1, 0, 1), repeat=3) if any(d)), key=lambda d: (not d[1], sum(map(abs, d))))
 LOWER = [d for d in DIRECTIONS if max(d) <= 0]
 
 
@@ -56,7 +57,7 @@
 
 
 def kernel(sizes, density, displacement, out, total_out, *scratch):
-    (field, g, b4, h, acc, rows, corner, nodes, hz, sd, last, energy,
+    (field, g, b4, acc, rows, corner, nodes, sd, energy,
      xs, ys, xys, zs, xzs, yzs, xyzs, xr, yr, xyr, zr, xzr, yzr, xyzr,
      dys, dxys, dzs, dxzs, dyzs, dxyzs, dzr, dxzr, dyzr, dxyzr, m6,
      part, part_in, send_sem, recv_sem, dsend_sem, drecv_sem, load_sem, psend_sem, precv_sem) = scratch
@@ -101,6 +102,19 @@
     load_nodes = pltpu.make_async_copy(displacement, nodes.at[:, pl.ds(0, ROWS)], load_sem.at[1])
     load_density.start()
     load_nodes.start()
+
+    barrier = pltpu.get_barrier_semaphore()
+    waits = 0
+    for partner, offsets, _ in stages:
+        for o in offsets:
+            pl.semaphore_signal(barrier, inc=1, device_id=partner(*o), device_id_type=MESH)
+        waits = waits + len(offsets)
+        if partner is partner_zc:
+            for d in DIRECTIONS:
+                @pl.when(inside(d))
+                def _(d=d):
+                    pl.semaphore_signal(barrier, inc=1, device_id=device(d), device_id_type=MESH)
+                waits = waits + inside(d).astype(jnp.int32)
 
     zero_row = jnp.zeros((8, NZ), F32)
 
@@ -139,18 +153,6 @@
             if d in lower:
                 zero(lower[d][1])
 
-    barrier = pltpu.get_barrier_semaphore()
-    waits = 0
-    for d in DIRECTIONS:
-        @pl.when(inside(d))
-        def _(d=d):
-            pl.semaphore_signal(barrier, inc=1, device_id=device(d), device_id_type=MESH)
-        waits = waits + inside(d).astype(jnp.int32)
-    for partner, offsets, _ in stages:
-        for o in offsets:
-            pl.semaphore_signal(barrier, inc=1, device_id=partner(*o), device_id_type=MESH)
-        waits = waits + len(offsets)
-
     def remote(source, target, send, recv, to):
         return pltpu.make_async_remote_copy(
             src_ref=source, dst_ref=target, send_sem=send, recv_sem=recv, device_id=to, device_id_type=MESH)
@@ -166,13 +168,9 @@
     for margin in (0, NY, (NX + 2) * NY, (NX + 3) * NY):
         field[pl.ds(margin, NY), :] = jnp.zeros((NY, NZ), F32)
 
-    def clear(i, _):
-        base = pl.multiple_of(i * YPAD, 16)
-        g[pl.ds(base, 8), :] = zero_row
-        g[pl.ds(base + 40, 8), :] = zero_row
-        return 0
-
-    lax.fori_loop(0, NX, clear, 0)
+    for i in range(NX):
+        g[pl.ds(i * YPAD, 8), :] = zero_row
+        g[pl.ds(i * YPAD + 40, 8), :] = zero_row
     for i in range(4):
         b4[pl.ds(i * YPAD, 8), :] = zero_row
         b4[pl.ds(i * YPAD + 40, 8), :] = zero_row
@@ -180,11 +178,13 @@
     zero(corner)
     zero(m6)
 
+    middle = jnp.zeros((112, 128), F32)
+
     def hat_rows(ref, base):
         at = [ref[pl.ds(base + 6 + k, NY), :] for k in range(5)]
         return 3.0 * at[2] + 2.0 * (at[1] + at[3]) + (at[0] + at[4])
 
-    def local_filter(p):
+    def local_filter(p, ref):
         for n, layer in enumerate((0, 1, NX - 2, NX - 1)):
             b4[pl.ds(n * YPAD + 8, NY), :] = field[pl.ds((layer + 2) * NY, NY), :]
         faces = [hat_rows(b4, n * YPAD) for n in range(4)]
@@ -195,12 +195,11 @@
             for sx in range(2):
                 xzs[p, sx, sz] = across(part_z, 1, 128, 32, 2 * sx - 1)
 
-        def x_pass(i, _):
-            at = [field[pl.ds(pl.multiple_of((i + k) * NY, NY), NY), :] for k in range(5)]
-            g[pl.ds(pl.multiple_of(i * YPAD, 16) + 8, NY), :] = 3.0 * at[2] + 2.0 * (at[1] + at[3]) + (at[0] + at[4])
-            return 0
-
-        lax.fori_loop(0, NX, x_pass, 0)
+        for t in range(NY // 8):
+            at = [field[pl.ds(i * NY + 8 * t, 8), :] for i in range(NX + 4)]
+            for i in range(NX):
+                g[pl.ds(i * YPAD + 8 + 8 * t, 8), :] = (
+                    3.0 * at[i + 2] + 2.0 * (at[i + 1] + at[i + 3]) + (at[i] + at[i + 4]))
 
         for n, row in enumerate((0, 1, NY - 2, NY - 1)):
             edge = g[pl.ds(8 + row, NX, stride=YPAD), :]
@@ -224,15 +223,10 @@
                 xyzs[p, 1, sy, sz] = jnp.where(lane < 8, both, 0.0)
                 xyzs[p, 0, sy, sz] = jnp.where(lane < 8, 0.0, both)
 
-        def y_pass(i, _):
-            v = hat_rows(g, pl.multiple_of(i * YPAD, 16))
-            h[pl.ds(pl.multiple_of(i * NY, NY), NY), :] = v
-            acc[pl.ds(pl.multiple_of(i * NY, NY), NY), :] = hat_lanes(v)
-            return 0
-
-        lax.fori_loop(0, NX, y_pass, 0)
         for k in range(GROUPS):
-            turned = h[pl.ds(k * 128, 128), :].T
+            v = jnp.concatenate([hat_rows(g, (4 * k + n) * YPAD) for n in range(4)], 0)
+            ref[pl.ds(k * 128, 128), :] = hat_lanes(v)
+            turned = v.T
             zs[p, 0, :, pl.ds(k * 128, 128)] = turned[0:8]
             zs[p, 1, :, pl.ds(k * 128, 128)] = turned[120:128]
 
@@ -242,11 +236,15 @@
             def _(d=d):
                 filter_copy(p, d).start()
 
-    def add_received(p):
+    def wait_received(p, along_y):
         for d in DIRECTIONS:
-            @pl.when(inside(tuple(-s for s in d)))
-            def _(d=d):
-                filter_copy(p, d).wait_recv()
+            if bool(d[1]) == along_y:
+                @pl.when(inside(tuple(-s for s in d)))
+                def _(d=d):
+                    filter_copy(p, d).wait_recv()
+
+    def add_xz(p, acc):
+        wait_received(p, False)
         def add(layer, v):
             acc[pl.ds(layer * NY, NY), :] = acc[pl.ds(layer * NY, NY), :] + v
 
@@ -256,9 +254,19 @@
         first, second = xr[p, 0, pl.ds(0, NY), :], xr[p, 0, pl.ds(NY, NY), :]
         add(NX - 2, first)
         add(NX - 1, 2.0 * first + second)
+        for k in range(GROUPS):
+            low, high = zr[p, 1, :, pl.ds(k * 128, 128)], zr[p, 0, :, pl.ds(k * 128, 128)]
+            if k == 0:
+                low, high = low + xzr[p, 1, 1], high + xzr[p, 1, 0]
+            if k == GROUPS - 1:
+                low, high = low + xzr[p, 0, 1], high + xzr[p, 0, 0]
+            turned = jnp.concatenate([across(low, 0, 8, 1, 1), middle, across(high, 0, 8, 1, -1)], 0).T
+            acc[pl.ds(k * 128, 128), :] = acc[pl.ds(k * 128, 128), :] + turned
+
+    def add_y(p, acc):
+        wait_received(p, True)
         low = sum([yzr[p, sy, 1] for sy in range(2)] + [xyzr[p, sx, sy, 1] for sx in range(2) for sy in range(2)])
         high = sum([yzr[p, sy, 0] for sy in range(2)] + [xyzr[p, sx, sy, 0] for sx in range(2) for sy in range(2)])
-        middle = jnp.zeros((112, 128), F32)
         turned = jnp.concatenate([across(low, 0, 8, 1, 1), middle, across(high, 0, 8, 1, -1)], 0).T
         at = {}
         for sy in range(2):
@@ -270,17 +278,9 @@
                 (0, at[1, 0] + 2.0 * at[1, 1]), (1, at[1, 1]), (NY - 2, at[0, 0]), (NY - 1, 2.0 * at[0, 0] + at[0, 1]))):
             place = pl.ds(row, NX, stride=NY)
             acc[place, :] = acc[place, :] + v + turned[n * 32:n * 32 + NX]
-        for k in range(GROUPS):
-            low, high = zr[p, 1, :, pl.ds(k * 128, 128)], zr[p, 0, :, pl.ds(k * 128, 128)]
-            if k == 0:
-                low, high = low + xzr[p, 1, 1], high + xzr[p, 1, 0]
-            if k == GROUPS - 1:
-                low, high = low + xzr[p, 0, 1], high + xzr[p, 0, 0]
-            turned = jnp.concatenate([across(low, 0, 8, 1, 1), middle, across(high, 0, 8, 1, -1)], 0).T
-            acc[pl.ds(k * 128, 128), :] = acc[pl.ds(k * 128, 128), :] + turned
 
     load_density.wait()
-    local_filter(0)
+    local_filter(0, acc)
     load_nodes.wait()
 
     def first_columns(v):
@@ -310,44 +310,32 @@
             lower_copy(d).start()
     send_filter(0)
 
-    for d in LOWER:
-        @pl.when(inside(tuple(-s for s in d)))
-        def _(d=d):
-            lower_copy(d).wait_recv()
+    def wait_lower(along_y):
+        for d in LOWER:
+            if bool(d[1]) == along_y:
+                @pl.when(inside(tuple(-s for s in d)))
+                def _(d=d):
+                    lower_copy(d).wait_recv()
+
     rest = jnp.zeros((120, 128), F32)
-    for k in range(GROUPS + 1):
-        if k < GROUPS:
-            packed = dzr[:, pl.ds(k * 128, 128)]
-        else:
-            packed = dxzr[...] + dyzr[...] + dxyzr[...]
-        turned = jnp.concatenate([packed, rest], 0).T
-        if k < GROUPS:
-            hz[pl.ds(k * 128, 128), :] = turned
-        else:
-            hz[pl.ds(k * 128, 64), :] = turned[:64]
-
-    def z_pass(base):
-        halo = hz[pl.ds(base, NY), :]
+
+    def z_pass(base, count, packed):
+        halo = jnp.concatenate([packed, rest], 0).T[:count]
         lane = iota(halo.shape, 1)
         out = []
         for m in range(3):
-            u = nodes[m, pl.ds(base, NY), :]
-            t = halo if m == 0 else pltpu.roll(halo, NZ - m, 1)
-            up = pltpu.roll(jnp.where(lane == 0, t, u), NZ - 1, 1)
+            u = nodes[m, pl.ds(base, count), :]
+            up = jnp.where(lane == NZ - 1, pltpu.roll(halo, NZ - 1 - m, 1), pltpu.roll(u, NZ - 1, 1))
             out += [u + up, up - u]
         return out
 
-    for k, v in enumerate(z_pass(ROWS + NY)):
-        last[k] = v
-
-    def z_layer(i, _):
-        base = pl.multiple_of(i * NODE_PAD, 8)
-        for k, v in enumerate(z_pass(pl.multiple_of(i * NY, NY))):
-            sd[k, pl.ds(base, NY), :] = v
-            sd[k, pl.ds(base + NY, 1), :] = last[k, pl.ds(i, 1), :]
-        return 0
-
-    lax.fori_loop(0, NX + 1, z_layer, 0)
+    wait_lower(False)
+    for k in range(GROUPS):
+        for n, v in enumerate(z_pass(k * 128, 128, dzr[:, pl.ds(k * 128, 128)])):
+            for i in range(4):
+                sd[n, pl.ds((4 * k + i) * NODE_PAD, NY), :] = v[i * NY:(i + 1) * NY]
+    for n, v in enumerate(z_pass(ROWS, NY, dxzr[...])):
+        sd[n, pl.ds(NX * NODE_PAD, NY), :] = v
 
     def yz_terms(i, t):
         base = pl.multiple_of(i * NODE_PAD, 8) + 8 * t
@@ -359,8 +347,8 @@
 
     square = lambda v: v * v
 
-    for t in range(NY // 8):
-        def element(i, before, t=t):
+    def energies(t):
+        def element(i, before):
             now = yz_terms(i, t)
             w = []
             for m in range(3):
@@ -377,11 +365,22 @@
             total += (SHEAR / 48) * (square(u[11] + v[101]) + square(v[101] + z[110]) + square(u[11] + z[110]))
             total += ((LAME + 4 * SHEAR) / 144) * (square(u[111]) + square(v[111]) + square(z[111]))
             energy[pl.ds(pl.multiple_of((i - 1) * NY, NY) + 8 * t, 8), :] = total
-            return tuple(now)
-
-        lax.fori_loop(1, NX + 1, element, tuple(yz_terms(0, t)))
-
-    add_received(0)
+            return now
+
+        def pair(n, before):
+            return tuple(element(2 * n + 2, element(2 * n + 1, before)))
+
+        lax.fori_loop(0, NX // 2, pair, tuple(yz_terms(0, t)))
+
+    for t in range(NY // 8 - 1):
+        energies(t)
+    add_xz(0, acc)
+    wait_lower(True)
+    for n, v in enumerate(z_pass(ROWS + NY, NY, pltpu.roll(dyzr[...] + dxyzr[...], 128 - NY, 1))):
+        sd[n, pl.ds(NY, NX + 1, stride=NODE_PAD), :] = v[:NX + 1]
+    energies(NY // 8 - 1)
+
+    add_y(0, acc)
 
     def inverse_cover(index, extent):
         end = extent - 1
@@ -391,15 +390,13 @@
     inverse_yz = inverse_cover(iota((NY, NZ), 0) + gy * NY, NY * size_y) * inverse_cover(
         iota((NY, NZ), 1) + gz * NZ, NZ * size_z)
 
-    def weigh(i, total):
-        base = pl.multiple_of(i * NY, NY)
+    total = jnp.zeros((NY, NZ), F32)
+    for i in range(NX):
         inverse = inverse_yz * inverse_cover(gx * NX + i, NX * size_x)
-        physical = acc[pl.ds(base, NY), :] * inverse
-        product = physical * physical * energy[pl.ds(base, NY), :]
-        field[pl.ds(base + 2 * NY, NY), :] = -3.0 * product * inverse
-        return total + physical * product
-
-    total = lax.fori_loop(0, NX, weigh, jnp.zeros((NY, NZ), F32))
+        physical = acc[pl.ds(i * NY, NY), :] * inverse
+        product = physical * physical * energy[pl.ds(i * NY, NY), :]
+        field[pl.ds((i + 2) * NY, NY), :] = -3.0 * product * inverse
+        total = total + physical * product
     total = jnp.sum(total, axis=0, keepdims=True)
 
     def send_total(s, value):
@@ -419,11 +416,11 @@
         return jnp.sum(part_in[s, 0:len(stages[s][1]) + 1], axis=0)
 
     send_total(0, total)
-    local_filter(1)
+    local_filter(1, out)
     send_filter(1)
     send_total(1, receive_total(0))
-    add_received(1)
-    out[...] = acc[...]
+    add_xz(1, out)
+    add_y(1, out)
     total = receive_total(1)
     total_out[...] = jnp.broadcast_to(jnp.sum(total, axis=1, keepdims=True), (8, 128))
 
@@ -443,9 +440,9 @@
     vmem = lambda *shape: pltpu.VMEM(shape, F32)
     partners = max(sizes[0] // sizes[3] * sizes[1], sizes[3] * sizes[2])
     scratch = [
-        vmem((NX + 4) * NY, NZ), vmem(NX * YPAD, NZ), vmem(4 * YPAD, NZ), vmem(ROWS, NZ), vmem(ROWS, NZ),
-        vmem(128, NZ), vmem(128, NZ), vmem(3, ROWS + 2 * NY, NZ), vmem(ROWS + 2 * NY, NZ),
-        vmem(6, (NX + 1) * NODE_PAD, NZ), vmem(6, NY, NZ), vmem(ROWS, NZ)]
+        vmem((NX + 4) * NY, NZ), vmem(NX * YPAD, NZ), vmem(4 * YPAD, NZ), vmem(ROWS, NZ),
+        vmem(128, NZ), vmem(128, NZ), vmem(3, ROWS + 2 * NY, NZ),
+        vmem(6, (NX + 1) * NODE_PAD, NZ), vmem(ROWS, NZ)]
     filters = [vmem(2, 2, 2 * NY, NZ), vmem(2, 2, 2, NX, NZ), vmem(2, 2, 2, 2, 8, NZ), vmem(2, 2, 8, ROWS),
                vmem(2, 2, 2, 8, 128), vmem(2, 2, 2, 8, 128), vmem(2, 2, 2, 2, 8, 128)]
     scratch += filters + filters
@@ -457,19 +454,27 @@
     return pl.pallas_call(
         functools.partial(kernel, sizes),
         out_shape=[jax.ShapeDtypeStruct((ROWS, NZ), F32), jax.ShapeDtypeStruct((8, 128), F32)],
-        in_specs=[pl.BlockSpec(memory_space=pl.ANY)] * 2,
+        in_specs=[pl.BlockSpec(memory_space=pltpu.HBM)] * 2,
         out_specs=[pl.BlockSpec(memory_space=pltpu.VMEM)] * 2,
         scratch_shapes=scratch,
         compiler_params=pltpu.CompilerParams(
-            collective_id=0, has_side_effects=True, vmem_limit_bytes=40 * 2**20),
+            collective_id=0, has_side_effects=True, vmem_limit_bytes=56_000_000),
         cost_estimate=pl.CostEstimate(flops=20_000_000, bytes_accessed=2_000_000, transcendentals=0),
     )(density, displacement)
 
 
-def scale_kernel(elements, field, total, out, mean_out):
+def scale_kernel(elements, field, total, out, mean_out, scaled, sem):
     mean = total[0:1, :] / elements
-    out[...] = field[...] / mean
     mean_out[...] = mean[:, 0:1]
+    inverse = 1.0 / mean
+    copies = []
+    for n in range(PARTS):
+        part = pl.ds(n * (ROWS // PARTS), ROWS // PARTS)
+        scaled[part, :] = field[part, :] * inverse
+        copies.append(pltpu.make_async_copy(scaled.at[part], out.at[part], sem.at[n]))
+        copies[-1].start()
+    for copy in copies:
+        copy.wait()
 
 
 def solution(mesh):
@@ -478,6 +483,10 @@
         sensitivity, mean = pl.pallas_call(
             functools.partial(scale_kernel, float(ROWS * NZ * mesh.size)),
             out_shape=[jax.ShapeDtypeStruct((ROWS, NZ), F32), jax.ShapeDtypeStruct((1, 1), F32)],
+            in_specs=[pl.BlockSpec(memory_space=pltpu.VMEM)] * 2,
+            out_specs=[pl.BlockSpec(memory_space=pl.ANY), pl.BlockSpec((1, 1), lambda: (0, 0))],
+            scratch_shapes=[pltpu.VMEM((ROWS, NZ), F32), pltpu.SemaphoreType.DMA((PARTS,))],
+            compiler_params=pltpu.CompilerParams(vmem_limit_bytes=4 * 2**20),
         )(filtered, total)
         return sensitivity.reshape(NX, NY, NZ), mean.reshape(())
 

time: 45.8 us -> 37 us (0.81)
  Pallas kernels: 41.3 us -> 36.3 us
  local copies, waits for them, and re-layouts: 3.59 us -> 0 us
    pallas_call x1, Pallas kernels: 39.6 us -> 35 us  [exchange(): pl.pallas_call(functools.partial(kernel, sizes), out_shape=[jax.ShapeDtyp...]
    unnamed x8 -> x0, local copies, waits for them, and re-layouts: 3.59 us -> none
    pallas_call x1, Pallas kernels: 1.78 us -> 1.3 us  [shards(): pl.pallas_call(functools.partial(scale_kernel, float(ROWS * NZ * mesh.siz...]
where the time goes in v2:
time: 37 us; the launch traced here: 36.9 us
  Pallas kernels  36.3 us (98%)
  between operations  0.64 us (2%)
    pallas_call x1, Pallas kernels, exchange(): pl.pallas_call(functools.partial(kernel, sizes), out_shape=[jax.ShapeDtyp...  35 us
    pallas_call x1, Pallas kernels, shards(): pl.pallas_call(functools.partial(scale_kernel, float(ROWS * NZ * mesh.siz...  1.3 us

profile of v2, /device:TPU:1, one launch (start us, length us, event | category | flops | bytes accessed | tf_op | source)
XLA Modules:
  0.0 36.9 jit_solution(363313145432533961)
XLA Ops:
  0.6 35.0 %shard_map.41 = (f32[768,128]{1,0:T(8,128)S(1)}, f32[8,128]{1,0:T(8,128)S(1)}) custom-call(f32[768,128]{1,0:T(8,128)} %bitcast.5, f32[3,768,128]{2,1,0:T(8,128)} %bitcast.4), custom_call_target="tpu_custom_call" | custom-call | flops 20000000 | bytes 2000000 | tf_op jit(solution)/shard_map/pallas_call | solution.py:454
  35.6 1.3 %shard_map.42 = (f32[768,128]{1,0:T(8,128)}, f32[1,1]{1,0:T(1,128)}) custom-call(f32[768,128]{1,0:T(8,128)S(1)} %get-tuple-element.6.field, f32[8,128]{1,0:T(8,128)S(1)} %get-tuple-element.7.total), custom_call_target="tpu_custom_call" | custom-call | tf_op jit(solution)/shard_map/pallas_call | solution.py:483

commit v3 on v2

--- a/solution.py
+++ b/solution.py
@@ -56,10 +56,18 @@
     return jnp.where(place == count - 1, two + 2.0 * one, jnp.where(place == count - 2, two, 0.0))
 
 
+def rows_at(places):
+    row = iota((8, NZ), 0)
+    tile = jnp.zeros((8, NZ), F32)
+    for place, value in places.items():
+        tile = jnp.where(row == place, jnp.broadcast_to(value, (8, NZ)), tile)
+    return tile
+
+
 def kernel(sizes, density, displacement, out, total_out, *scratch):
     (field, g, b4, acc, rows, corner, nodes, sd, energy,
      xs, ys, xys, zs, xzs, yzs, xyzs, xr, yr, xyr, zr, xzr, yzr, xyzr,
-     dys, dxys, dzs, dxzs, dyzs, dxyzs, dzr, dxzr, dyzr, dxyzr, m6,
+     dys, dxys, dzs, dxzs, dyzs, dxyzs, dxyr, dzr, dxzr, dyzr, dxyzr, m6,
      part, part_in, send_sem, recv_sem, dsend_sem, drecv_sem, load_sem, psend_sem, precv_sem) = scratch
     size_x, size_y, size_z, ring_y = sizes
     gx, gy, gz = (lax.axis_index(a) for a in ("gx", "gy", "gz"))
@@ -81,22 +89,27 @@
     my_core = lax.rem(gy, 2)
     count_z = layers_z * (size_y // 2)
 
-    def partner_zc(dz, dc):
-        z, c = lax.rem(my_z + dz, count_z), lax.rem(my_core + dc, 2)
+    halves = size_y // 2
+    early = gy < 2
+
+    def at_zc(z, c):
         return (lax.rem(z, layers_z) * ring_y + my_y, (z // layers_z) * 2 + c, gz)
 
     def partner_xy(dx, dy):
         x, y = lax.rem(gz + dx, size_z), lax.rem(my_y + dy, ring_y)
         return ((gx // ring_y) * ring_y + y, gy, x)
 
+    mirror = at_zc(count_z - 1 - my_z, my_core)
+    column = [(z, c) for z in range(layers_z) for c in range(2)]
+
+    def other(z, c):
+        return jnp.logical_or(my_z != z, my_core != c)
+
     def far_first(counts):
         offs = [o for o in itertools.product(*[range(c) for c in counts]) if any(o)]
         return sorted(offs, key=lambda o: -sum(min(s, c - s) for s, c in zip(o, counts)))
 
-    stages = [
-        (partner_zc, far_first((count_z, 2)), my_z * 2 + my_core),
-        (partner_xy, far_first((size_z, ring_y)), gz * ring_y + my_y),
-    ]
+    plane = far_first((size_z, ring_y))
 
     load_density = pltpu.make_async_copy(density, field.at[pl.ds(2 * NY, ROWS)], load_sem.at[0])
     load_nodes = pltpu.make_async_copy(displacement, nodes.at[:, pl.ds(0, ROWS)], load_sem.at[1])
@@ -104,17 +117,32 @@
     load_nodes.start()
 
     barrier = pltpu.get_barrier_semaphore()
+
+    def greet(to):
+        pl.semaphore_signal(barrier, inc=1, device_id=to, device_id_type=MESH)
+
     waits = 0
-    for partner, offsets, _ in stages:
-        for o in offsets:
-            pl.semaphore_signal(barrier, inc=1, device_id=partner(*o), device_id_type=MESH)
-        waits = waits + len(offsets)
-        if partner is partner_zc:
-            for d in DIRECTIONS:
-                @pl.when(inside(d))
-                def _(d=d):
-                    pl.semaphore_signal(barrier, inc=1, device_id=device(d), device_id_type=MESH)
-                waits = waits + inside(d).astype(jnp.int32)
+    for d in DIRECTIONS:
+        @pl.when(inside(d))
+        def _(d=d):
+            greet(device(d))
+        waits = waits + inside(d).astype(jnp.int32)
+
+    @pl.when(early)
+    def _():
+        for z, c in [(z, c) for z in range(count_z) for c in range(2)]:
+            @pl.when(other(z, c))
+            def _(z=z, c=c):
+                greet(at_zc(z, c))
+        for o in plane:
+            greet(partner_xy(*o))
+
+    if halves > 1:
+        @pl.when(jnp.logical_not(early))
+        def _():
+            greet(mirror)
+
+    waits = waits + jnp.where(early, 2 * layers_z - 1 + len(plane) + (halves - 1), 2 * layers_z)
 
     zero_row = jnp.zeros((8, NZ), F32)
 
@@ -138,7 +166,7 @@
     lower = {
         (-1, 0, 0): (nodes.at[:, pl.ds(0, NY)], nodes.at[:, pl.ds(ROWS, NY)]),
         (0, -1, 0): (dys, nodes.at[:, pl.ds(ROWS + NY, NX)]),
-        (-1, -1, 0): (dxys, nodes.at[:, pl.ds(ROWS + NY + NX, 8)]),
+        (-1, -1, 0): (dxys, dxyr),
         (0, 0, -1): (dzs, dzr),
         (-1, 0, -1): (dxzs, dxzr),
         (0, -1, -1): (dyzs, dyzr),
@@ -184,6 +212,15 @@
         at = [ref[pl.ds(base + 6 + k, NY), :] for k in range(5)]
         return 3.0 * at[2] + 2.0 * (at[1] + at[3]) + (at[0] + at[4])
 
+    def store_pair(ref, tile, first):
+        ref[0] = tile[first:first + 1]
+        ref[1] = tile[first + 1:first + 2]
+
+    def z_edges(low, high):
+        return jnp.concatenate([
+            rows_at({0: low[0] + 2.0 * low[1], 1: low[1]}), middle,
+            rows_at({6: high[0], 7: 2.0 * high[0] + high[1]})], 0).T
+
     def local_filter(p, ref):
         for n, layer in enumerate((0, 1, NX - 2, NX - 1)):
             b4[pl.ds(n * YPAD + 8, NY), :] = field[pl.ds((layer + 2) * NY, NY), :]
@@ -193,7 +230,7 @@
         turned = jnp.concatenate(faces, 0).T
         for sz, part_z in enumerate((turned[0:8], turned[120:128])):
             for sx in range(2):
-                xzs[p, sx, sz] = across(part_z, 1, 128, 32, 2 * sx - 1)
+                store_pair(xzs.at[p, sx, sz], across(part_z, 1, 128, 32, 2 * sx - 1), 6 * sz)
 
         for t in range(NY // 8):
             at = [field[pl.ds(i * NY + 8 * t, 8), :] for i in range(NX + 4)]
@@ -209,26 +246,26 @@
             up, down = across(raw[NX - 8:], 0, 8, 1, 1), across(raw[:8], 0, 8, 1, -1)
             corner[pl.ds(n * 32, 8), :] = up
             corner[pl.ds(n * 32 + NX - 8, 8), :] = down
-            xys[p, 1, n // 2, n % 2] = hat_lanes(up)
-            xys[p, 0, n // 2, n % 2] = hat_lanes(down)
+            store_pair(xys.at[p, 1, n // 2, pl.ds(2 * (n % 2), 2)], hat_lanes(up), 0)
+            store_pair(xys.at[p, 0, n // 2, pl.ds(2 * (n % 2), 2)], hat_lanes(down), 6)
         turned = rows[...].T
         for sz, part_z in enumerate((turned[0:8], turned[120:128])):
             for sy in range(2):
-                yzs[p, sy, sz] = across(part_z, 1, 128, 32, 2 * sy - 1)
+                store_pair(yzs.at[p, sy, sz], across(part_z, 1, 128, 32, 2 * sy - 1), 6 * sz)
         turned = corner[...].T
         lane = lax.rem(iota((8, 128), 1), 32)
         for sz, part_z in enumerate((turned[0:8], turned[120:128])):
             for sy in range(2):
                 both = across(part_z, 1, 128, 32, 2 * sy - 1)
-                xyzs[p, 1, sy, sz] = jnp.where(lane < 8, both, 0.0)
-                xyzs[p, 0, sy, sz] = jnp.where(lane < 8, 0.0, both)
+                store_pair(xyzs.at[p, 1, sy, sz], jnp.where(lane < 8, both, 0.0), 6 * sz)
+                store_pair(xyzs.at[p, 0, sy, sz], jnp.where(lane < 8, 0.0, both), 6 * sz)
 
         for k in range(GROUPS):
             v = jnp.concatenate([hat_rows(g, (4 * k + n) * YPAD) for n in range(4)], 0)
             ref[pl.ds(k * 128, 128), :] = hat_lanes(v)
             turned = v.T
-            zs[p, 0, :, pl.ds(k * 128, 128)] = turned[0:8]
-            zs[p, 1, :, pl.ds(k * 128, 128)] = turned[120:128]
+            store_pair(zs.at[p, 0, pl.ds(2 * k, 2)], turned[0:8], 0)
+            store_pair(zs.at[p, 1, pl.ds(2 * k, 2)], turned[120:128], 6)
 
     def send_filter(p):
         for d in DIRECTIONS:
@@ -255,25 +292,25 @@
         add(NX - 2, first)
         add(NX - 1, 2.0 * first + second)
         for k in range(GROUPS):
-            low, high = zr[p, 1, :, pl.ds(k * 128, 128)], zr[p, 0, :, pl.ds(k * 128, 128)]
-            if k == 0:
-                low, high = low + xzr[p, 1, 1], high + xzr[p, 1, 0]
-            if k == GROUPS - 1:
-                low, high = low + xzr[p, 0, 1], high + xzr[p, 0, 0]
-            turned = jnp.concatenate([across(low, 0, 8, 1, 1), middle, across(high, 0, 8, 1, -1)], 0).T
-            acc[pl.ds(k * 128, 128), :] = acc[pl.ds(k * 128, 128), :] + turned
+            low, high = [[zr[p, sz, 2 * k + i] for i in range(2)] for sz in (1, 0)]
+            edge = {0: 1, GROUPS - 1: 0}.get(k)
+            if edge is not None:
+                low, high = [[v[i] + xzr[p, edge, sz, i] for i in range(2)] for v, sz in ((low, 1), (high, 0))]
+            acc[pl.ds(k * 128, 128), :] = acc[pl.ds(k * 128, 128), :] + z_edges(low, high)
 
     def add_y(p, acc):
         wait_received(p, True)
-        low = sum([yzr[p, sy, 1] for sy in range(2)] + [xyzr[p, sx, sy, 1] for sx in range(2) for sy in range(2)])
-        high = sum([yzr[p, sy, 0] for sy in range(2)] + [xyzr[p, sx, sy, 0] for sx in range(2) for sy in range(2)])
-        turned = jnp.concatenate([across(low, 0, 8, 1, 1), middle, across(high, 0, 8, 1, -1)], 0).T
+        low, high = [[sum([yzr[p, sy, sz, i] for sy in range(2)] + [
+            xyzr[p, sx, sy, sz, i] for sx in range(2) for sy in range(2)]) for i in range(2)] for sz in (1, 0)]
+        turned = z_edges(low, high)
         at = {}
         for sy in range(2):
             for n in range(2):
                 center = yr[p, sy, n]
-                at[sy, n] = jnp.concatenate(
-                    [center[:8] + xyr[p, 1, sy, n], center[8:16], center[16:] + xyr[p, 0, sy, n]], 0)
+                up, down = [[xyr[p, sx, sy, 2 * n + i] for i in range(2)] for sx in (1, 0)]
+                at[sy, n] = jnp.concatenate([
+                    center[:8] + rows_at({0: up[0], 1: up[1]}), center[8:16],
+                    center[16:] + rows_at({6: down[0], 7: down[1]})], 0)
         for n, (row, v) in enumerate((
                 (0, at[1, 0] + 2.0 * at[1, 1]), (1, at[1, 1]), (NY - 2, at[0, 0]), (NY - 1, 2.0 * at[0, 0] + at[0, 1]))):
             place = pl.ds(row, NX, stride=NY)
@@ -290,18 +327,23 @@
 
     for m in range(3):
         dys[m] = nodes[m, pl.ds(0, NX, stride=NY), :]
-        dxys[m] = dys[m, pl.ds(0, 8), :]
+        dxys[m] = dys[m, pl.ds(0, 1), :]
     for k in range(GROUPS):
         columns = first_columns([nodes[m, pl.ds(k * 128, 128), :] for m in range(3)])
-        dzs[:, pl.ds(k * 128, 128)] = columns.T[0:8]
+        turned = columns.T[0:8]
+        for m in range(3):
+            dzs[3 * k + m] = turned[m:m + 1]
         if k == 0:
             m6[pl.ds(0, NY), :] = columns[:NY]
     m6[pl.ds(NY, NX), :] = first_columns([dys[m] for m in range(3)])
     turned = m6[...].T[0:8]
     lane8 = iota((8, 128), 1)
-    dxzs[...] = jnp.where(lane8 < NY, turned, 0.0)
-    dyzs[...] = jnp.where(jnp.logical_and(lane8 >= NY, lane8 < NY + NX), turned, 0.0)
-    dxyzs[...] = jnp.where(lane8 == NY + NX, pltpu.roll(turned, NY + NX, 1), 0.0)
+    for target, tile in (
+            (dxzs, jnp.where(lane8 < NY, turned, 0.0)),
+            (dyzs, jnp.where(jnp.logical_and(lane8 >= NY, lane8 < NY + NX), turned, 0.0)),
+            (dxyzs, jnp.where(lane8 == NY + NX, pltpu.roll(turned, NY + NX, 1), 0.0))):
+        for m in range(3):
+            target[m] = tile[m:m + 1]
 
     pl.semaphore_wait(barrier, waits)
     for d in LOWER:
@@ -320,7 +362,7 @@
     rest = jnp.zeros((120, 128), F32)
 
     def z_pass(base, count, packed):
-        halo = jnp.concatenate([packed, rest], 0).T[:count]
+        halo = jnp.concatenate([rows_at(dict(enumerate(packed))), rest], 0).T[:count]
         lane = iota(halo.shape, 1)
         out = []
         for m in range(3):
@@ -331,10 +373,10 @@
 
     wait_lower(False)
     for k in range(GROUPS):
-        for n, v in enumerate(z_pass(k * 128, 128, dzr[:, pl.ds(k * 128, 128)])):
+        for n, v in enumerate(z_pass(k * 128, 128, [dzr[3 * k + m] for m in range(3)])):
             for i in range(4):
                 sd[n, pl.ds((4 * k + i) * NODE_PAD, NY), :] = v[i * NY:(i + 1) * NY]
-    for n, v in enumerate(z_pass(ROWS, NY, dxzr[...])):
+    for n, v in enumerate(z_pass(ROWS, NY, [dxzr[m] for m in range(3)])):
         sd[n, pl.ds(NX * NODE_PAD, NY), :] = v
 
     def yz_terms(i, t):
@@ -376,7 +418,9 @@
         energies(t)
     add_xz(0, acc)
     wait_lower(True)
-    for n, v in enumerate(z_pass(ROWS + NY, NY, pltpu.roll(dyzr[...] + dxyzr[...], 128 - NY, 1))):
+    for m in range(3):
+        nodes[m, pl.ds(ROWS + NY + NX, 1), :] = dxyr[m]
+    for n, v in enumerate(z_pass(ROWS + NY, NY, [pltpu.roll(dyzr[m] + dxyzr[m], 128 - NY, 1) for m in range(3)])):
         sd[n, pl.ds(NY, NX + 1, stride=NODE_PAD), :] = v[:NX + 1]
     energies(NY // 8 - 1)
 
@@ -399,30 +443,55 @@
         total = total + physical * product
     total = jnp.sum(total, axis=0, keepdims=True)
 
-    def send_total(s, value):
-        partner, offsets, mine = stages[s]
-        part[s] = value
-        part_in[s, mine] = value
-        for o in offsets:
-            remote(part.at[s], part_in.at[s, mine], psend_sem.at[s], precv_sem.at[s], partner(*o)).start()
-
-    def total_wait(s, sem):
-        n = len(stages[s][1])
+    def sum_copy(s, mine, to):
+        return remote(part.at[s], part_in.at[s, mine], psend_sem.at[s], precv_sem.at[s], to)
+
+    def sum_wait(sem, s, n):
         whole = part_in.at[s, pl.ds(0, n)]
         pltpu.make_async_copy(whole, whole, sem.at[s]).wait()
 
-    def receive_total(s):
-        total_wait(s, precv_sem)
-        return jnp.sum(part_in[s, 0:len(stages[s][1]) + 1], axis=0)
-
-    send_total(0, total)
+    mine = my_z * 2 + my_core
+    part[0] = total
+    for z, c in column:
+        @pl.when(other(z, c))
+        def _(z=z, c=c):
+            sum_copy(0, mine, at_zc(z, c)).start()
     local_filter(1, out)
     send_filter(1)
-    send_total(1, receive_total(0))
+
+    @pl.when(early)
+    def _():
+        part_in[0, mine] = total
+        sum_wait(precv_sem, 0, 2 * count_z - 1)
+        partial = jnp.sum(part_in[0, 0:2 * count_z], axis=0)
+        here = gz * ring_y + my_y
+        part[1] = partial
+        part_in[1, here] = partial
+        for o in plane:
+            sum_copy(1, here, partner_xy(*o)).start()
+
     add_xz(1, out)
     add_y(1, out)
-    total = receive_total(1)
-    total_out[...] = jnp.broadcast_to(jnp.sum(total, axis=1, keepdims=True), (8, 128))
+
+    @pl.when(early)
+    def _():
+        sum_wait(precv_sem, 1, len(plane))
+        final = jnp.sum(part_in[1, 0:len(plane) + 1], axis=0)
+        part[2] = final
+        if halves > 1:
+            sum_copy(2, 0, mirror).start()
+            sum_copy(2, 0, mirror).wait_send()
+        sum_wait(psend_sem, 1, len(plane))
+        sum_wait(psend_sem, 0, 2 * layers_z - 1)
+
+    @pl.when(jnp.logical_not(early))
+    def _():
+        if halves > 1:
+            sum_wait(precv_sem, 2, 1)
+            part[2] = part_in[2, 0]
+        sum_wait(psend_sem, 0, 2 * layers_z)
+
+    total_out[...] = jnp.broadcast_to(jnp.sum(part[2], axis=1, keepdims=True), (8, 128))
 
     for d in DIRECTIONS:
         @pl.when(inside(d))
@@ -431,8 +500,6 @@
                 filter_copy(p, d).wait_send()
             if d in lower:
                 lower_copy(d).wait_send()
-    for s in range(2):
-        total_wait(s, psend_sem)
 
 
 def exchange(mesh, density, displacement):
@@ -443,14 +510,14 @@
         vmem((NX + 4) * NY, NZ), vmem(NX * YPAD, NZ), vmem(4 * YPAD, NZ), vmem(ROWS, NZ),
         vmem(128, NZ), vmem(128, NZ), vmem(3, ROWS + 2 * NY, NZ),
         vmem(6, (NX + 1) * NODE_PAD, NZ), vmem(ROWS, NZ)]
-    filters = [vmem(2, 2, 2 * NY, NZ), vmem(2, 2, 2, NX, NZ), vmem(2, 2, 2, 2, 8, NZ), vmem(2, 2, 8, ROWS),
-               vmem(2, 2, 2, 8, 128), vmem(2, 2, 2, 8, 128), vmem(2, 2, 2, 2, 8, 128)]
+    filters = [vmem(2, 2, 2 * NY, NZ), vmem(2, 2, 2, NX, NZ), vmem(2, 2, 2, 4, 1, NZ), vmem(2, 2, 2 * GROUPS, 1, 128),
+               vmem(2, 2, 2, 2, 1, 128), vmem(2, 2, 2, 2, 1, 128), vmem(2, 2, 2, 2, 2, 1, 128)]
     scratch += filters + filters
-    scratch += [vmem(3, NX, NZ), vmem(3, 8, NZ), vmem(8, ROWS), vmem(8, 128), vmem(8, 128), vmem(8, 128),
-                vmem(8, ROWS), vmem(8, 128), vmem(8, 128), vmem(8, 128), vmem(128, 128)]
-    scratch += [vmem(2, 1, 128), vmem(2, partners, 1, 128)]
+    edges = [vmem(3, 1, NZ), vmem(3 * GROUPS, 1, 128), vmem(3, 1, 128), vmem(3, 1, 128), vmem(3, 1, 128)]
+    scratch += [vmem(3, NX, NZ)] + edges + edges + [vmem(128, 128)]
+    scratch += [vmem(3, 1, 128), vmem(3, partners, 1, 128)]
     dma = pltpu.SemaphoreType.DMA
-    scratch += [dma((2, 27)), dma((2, 27)), dma((8,)), dma((8,)), dma((2,)), dma((2,)), dma((2,))]
+    scratch += [dma((2, 27)), dma((2, 27)), dma((8,)), dma((8,)), dma((2,)), dma((3,)), dma((3,))]
     return pl.pallas_call(
         functools.partial(kernel, sizes),
         out_shape=[jax.ShapeDtypeStruct((ROWS, NZ), F32), jax.ShapeDtypeStruct((8, 128), F32)],

time: 37 us -> 35.6 us (0.962)
  Pallas kernels: 36.3 us -> 34.8 us
    pallas_call x1, Pallas kernels: 35 us -> 33.5 us  [exchange(): pl.pallas_call(functools.partial(kernel, sizes), out_shape=[jax.ShapeDtyp...]
where the time goes in v3:
time: 35.6 us; the launch traced here: 35.5 us
  Pallas kernels  34.8 us (98%)
  between operations  0.64 us (2%)
    pallas_call x1, Pallas kernels, exchange(): pl.pallas_call(functools.partial(kernel, sizes), out_shape=[jax.ShapeDtyp...  33.5 us
    pallas_call x1, Pallas kernels, shards(): pl.pallas_call(functools.partial(scale_kernel, float(ROWS * NZ * mesh.siz...  1.3 us

profile of v3, /device:TPU:1, one launch (start us, length us, event | category | flops | bytes accessed | tf_op | source)
XLA Modules:
  0.0 35.5 jit_solution(11480500650957575421)
XLA Ops:
  0.6 33.5 %shard_map.41 = (f32[768,128]{1,0:T(8,128)S(1)}, f32[8,128]{1,0:T(8,128)S(1)}) custom-call(f32[768,128]{1,0:T(8,128)} %bitcast.5, f32[3,768,128]{2,1,0:T(8,128)} %bitcast.4), custom_call_target="tpu_custom_call" | custom-call | flops 20000000 | bytes 2000000 | tf_op jit(solution)/shard_map/pallas_call | solution.py:521
  34.2 1.3 %shard_map.42 = (f32[768,128]{1,0:T(8,128)}, f32[1,1]{1,0:T(1,128)}) custom-call(f32[768,128]{1,0:T(8,128)S(1)} %get-tuple-element.6.field, f32[8,128]{1,0:T(8,128)S(1)} %get-tuple-element.7.total), custom_call_target="tpu_custom_call" | custom-call | tf_op jit(solution)/shard_map/pallas_call | solution.py:550

commit v4 on v3

--- a/solution.py
+++ b/solution.py
@@ -68,7 +68,7 @@
     (field, g, b4, acc, rows, corner, nodes, sd, energy,
      xs, ys, xys, zs, xzs, yzs, xyzs, xr, yr, xyr, zr, xzr, yzr, xyzr,
      dys, dxys, dzs, dxzs, dyzs, dxyzs, dxyr, dzr, dxzr, dyzr, dxyzr, m6,
-     part, part_in, send_sem, recv_sem, dsend_sem, drecv_sem, load_sem, psend_sem, precv_sem) = scratch
+     part, part_in, send_sem, recv_sem, dsend_sem, drecv_sem, load_sem, psend_sem, precv_sem, pass_sem) = scratch
     size_x, size_y, size_z, ring_y = sizes
     gx, gy, gz = (lax.axis_index(a) for a in ("gx", "gy", "gz"))
 
@@ -99,7 +99,12 @@
         x, y = lax.rem(gz + dx, size_z), lax.rem(my_y + dy, ring_y)
         return ((gx // ring_y) * ring_y + y, gy, x)
 
-    mirror = at_zc(count_z - 1 - my_z, my_core)
+    server = layers_z - 1 - (my_z - layers_z) // 2
+    serves = [z for z in range(layers_z, count_z)]
+
+    def served_from(z):
+        return layers_z - 1 - (z - layers_z) // 2
+
     column = [(z, c) for z in range(layers_z) for c in range(2)]
 
     def other(z, c):
@@ -140,9 +145,10 @@
     if halves > 1:
         @pl.when(jnp.logical_not(early))
         def _():
-            greet(mirror)
-
-    waits = waits + jnp.where(early, 2 * layers_z - 1 + len(plane) + (halves - 1), 2 * layers_z)
+            greet(at_zc(server, my_core))
+
+    served = sum((my_z == served_from(z)).astype(jnp.int32) for z in serves) if serves else 0
+    waits = waits + jnp.where(early, 2 * layers_z - 1 + len(plane) + served, 2 * layers_z)
 
     zero_row = jnp.zeros((8, NZ), F32)
 
@@ -473,26 +479,6 @@
     add_xz(1, out)
     add_y(1, out)
 
-    @pl.when(early)
-    def _():
-        sum_wait(precv_sem, 1, len(plane))
-        final = jnp.sum(part_in[1, 0:len(plane) + 1], axis=0)
-        part[2] = final
-        if halves > 1:
-            sum_copy(2, 0, mirror).start()
-            sum_copy(2, 0, mirror).wait_send()
-        sum_wait(psend_sem, 1, len(plane))
-        sum_wait(psend_sem, 0, 2 * layers_z - 1)
-
-    @pl.when(jnp.logical_not(early))
-    def _():
-        if halves > 1:
-            sum_wait(precv_sem, 2, 1)
-            part[2] = part_in[2, 0]
-        sum_wait(psend_sem, 0, 2 * layers_z)
-
-    total_out[...] = jnp.broadcast_to(jnp.sum(part[2], axis=1, keepdims=True), (8, 128))
-
     for d in DIRECTIONS:
         @pl.when(inside(d))
         def _(d=d):
@@ -500,6 +486,35 @@
                 filter_copy(p, d).wait_send()
             if d in lower:
                 lower_copy(d).wait_send()
+
+    @pl.when(early)
+    def _():
+        sum_wait(psend_sem, 0, 2 * layers_z - 1)
+        sum_wait(psend_sem, 1, len(plane))
+        sum_wait(precv_sem, 1, len(plane))
+        part[2] = jnp.sum(part_in[1, 0:len(plane) + 1], axis=0)
+
+    def pass_on(z):
+        return remote(part.at[2], part_in.at[2, 0], pass_sem.at[z - layers_z], precv_sem.at[2], at_zc(z, my_core))
+
+    for z in serves:
+        @pl.when(my_z == served_from(z))
+        def _(z=z):
+            pass_on(z).start()
+
+    @pl.when(jnp.logical_not(early))
+    def _():
+        sum_wait(psend_sem, 0, 2 * layers_z)
+        if halves > 1:
+            sum_wait(precv_sem, 2, 1)
+            part[2] = part_in[2, 0]
+
+    total_out[...] = jnp.broadcast_to(jnp.sum(part[2], axis=1, keepdims=True), (8, 128))
+
+    for z in serves:
+        @pl.when(my_z == served_from(z))
+        def _(z=z):
+            pass_on(z).wait_send()
 
 
 def exchange(mesh, density, displacement):
@@ -517,7 +532,7 @@
     scratch += [vmem(3, NX, NZ)] + edges + edges + [vmem(128, 128)]
     scratch += [vmem(3, 1, 128), vmem(3, partners, 1, 128)]
     dma = pltpu.SemaphoreType.DMA
-    scratch += [dma((2, 27)), dma((2, 27)), dma((8,)), dma((8,)), dma((2,)), dma((3,)), dma((3,))]
+    scratch += [dma((2, 27)), dma((2, 27)), dma((8,)), dma((8,)), dma((2,)), dma((3,)), dma((3,)), dma((8,))]
     return pl.pallas_call(
         functools.partial(kernel, sizes),
         out_shape=[jax.ShapeDtypeStruct((ROWS, NZ), F32), jax.ShapeDtypeStruct((8, 128), F32)],
@@ -530,11 +545,12 @@
     )(density, displacement)
 
 
-def scale_kernel(elements, field, total, out, mean_out, scaled, sem):
+def scale_kernel(elements, field, total, out, mean_out, scaled, mean_ref, sem):
     mean = total[0:1, :] / elements
-    mean_out[...] = mean[:, 0:1]
+    mean_ref[...] = mean[:, 0:1]
     inverse = 1.0 / mean
-    copies = []
+    copies = [pltpu.make_async_copy(mean_ref, mean_out, sem.at[PARTS])]
+    copies[0].start()
     for n in range(PARTS):
         part = pl.ds(n * (ROWS // PARTS), ROWS // PARTS)
         scaled[part, :] = field[part, :] * inverse
@@ -551,8 +567,9 @@
             functools.partial(scale_kernel, float(ROWS * NZ * mesh.size)),
             out_shape=[jax.ShapeDtypeStruct((ROWS, NZ), F32), jax.ShapeDtypeStruct((1, 1), F32)],
             in_specs=[pl.BlockSpec(memory_space=pltpu.VMEM)] * 2,
-            out_specs=[pl.BlockSpec(memory_space=pl.ANY), pl.BlockSpec((1, 1), lambda: (0, 0))],
-            scratch_shapes=[pltpu.VMEM((ROWS, NZ), F32), pltpu.SemaphoreType.DMA((PARTS,))],
+            out_specs=[pl.BlockSpec(memory_space=pl.ANY)] * 2,
+            scratch_shapes=[
+                pltpu.VMEM((ROWS, NZ), F32), pltpu.VMEM((1, 1), F32), pltpu.SemaphoreType.DMA((PARTS + 1,))],
             compiler_params=pltpu.CompilerParams(vmem_limit_bytes=4 * 2**20),
         )(filtered, total)
         return sensitivity.reshape(NX, NY, NZ), mean.reshape(())

time: 35.6 us -> 34.4 us (0.966)
  Pallas kernels: 34.8 us -> 33.6 us
    pallas_call x1, Pallas kernels: 33.5 us -> 32.8 us  [exchange(): pl.pallas_call(functools.partial(kernel, sizes), out_shape=[jax.ShapeDtyp...]
    pallas_call x1, Pallas kernels: 1.3 us -> 0.8 us  [shards(): pl.pallas_call(functools.partial(scale_kernel, float(ROWS * NZ * mesh.siz...]
where the time goes in v4:
time: 34.4 us; the launch traced here: 34.2 us
  Pallas kernels  33.6 us (98%)
  between operations  0.64 us (2%)
    pallas_call x1, Pallas kernels, exchange(): pl.pallas_call(functools.partial(kernel, sizes), out_shape=[jax.ShapeDtyp...  32.8 us
    pallas_call x1, Pallas kernels, shards(): pl.pallas_call(functools.partial(scale_kernel, float(ROWS * NZ * mesh.siz...  0.8 us

profile of v4, /device:TPU:1, one launch (start us, length us, event | category | flops | bytes accessed | tf_op | source)
XLA Modules:
  0.0 34.2 jit_solution(13668519568623096622)
XLA Ops:
  0.6 32.8 %shard_map.41 = (f32[768,128]{1,0:T(8,128)S(1)}, f32[8,128]{1,0:T(8,128)S(1)}) custom-call(f32[768,128]{1,0:T(8,128)} %bitcast.5, f32[3,768,128]{2,1,0:T(8,128)} %bitcast.4), custom_call_target="tpu_custom_call" | custom-call | flops 20000000 | bytes 2000000 | tf_op jit(solution)/shard_map/pallas_call | solution.py:536
  33.4 0.8 %shard_map.42 = (f32[768,128]{1,0:T(8,128)}, f32[1,1]{1,0:T(1,128)}) custom-call(f32[768,128]{1,0:T(8,128)S(1)} %get-tuple-element.6.field, f32[8,128]{1,0:T(8,128)S(1)} %get-tuple-element.7.total), custom_call_target="tpu_custom_call" | custom-call | tf_op jit(solution)/shard_map/pallas_call | solution.py:566

commit v5 on v4

--- a/solution.py
+++ b/solution.py
@@ -19,7 +19,7 @@
 LAME = 0.3 / (1.3 * 0.4)
 SHEAR = 1.0 / 2.6
 
-DIRECTIONS = sorted((d for d in itertools.product((-1, 0, 1), repeat=3) if any(d)), key=lambda d: (not d[1], sum(map(abs, d))))
+DIRECTIONS = sorted((d for d in itertools.product((-1, 0, 1), repeat=3) if any(d)), key=lambda d: (not d[1], -sum(map(abs, d))))
 LOWER = [d for d in DIRECTIONS if max(d) <= 0]
 
 
@@ -100,10 +100,10 @@
         return ((gx // ring_y) * ring_y + y, gy, x)
 
     server = layers_z - 1 - (my_z - layers_z) // 2
-    serves = [z for z in range(layers_z, count_z)]
-
-    def served_from(z):
-        return layers_z - 1 - (z - layers_z) // 2
+    serves = [(z, c) for z in range(layers_z, count_z) for c in range(2)]
+
+    def serving(z):
+        return jnp.logical_and(my_z == layers_z - 1 - (z - layers_z) // 2, my_core == 1)
 
     column = [(z, c) for z in range(layers_z) for c in range(2)]
 
@@ -145,9 +145,9 @@
     if halves > 1:
         @pl.when(jnp.logical_not(early))
         def _():
-            greet(at_zc(server, my_core))
-
-    served = sum((my_z == served_from(z)).astype(jnp.int32) for z in serves) if serves else 0
+            greet(at_zc(server, 1))
+
+    served = sum(serving(z).astype(jnp.int32) for z, _ in serves) if serves else 0
     waits = waits + jnp.where(early, 2 * layers_z - 1 + len(plane) + served, 2 * layers_z)
 
     zero_row = jnp.zeros((8, NZ), F32)
@@ -273,14 +273,28 @@
             store_pair(zs.at[p, 0, pl.ds(2 * k, 2)], turned[0:8], 0)
             store_pair(zs.at[p, 1, pl.ds(2 * k, 2)], turned[120:128], 6)
 
-    def send_filter(p):
+    def send_filter(p, along_y, when=None, faces=(True, False)):
         for d in DIRECTIONS:
-            @pl.when(inside(d))
-            def _(d=d):
-                filter_copy(p, d).start()
+            if d[1] == along_y and (d == (0, along_y, 0)) in faces:
+                go = inside(d) if when is None else jnp.logical_and(inside(d), when)
+
+                @pl.when(go)
+                def _(d=d):
+                    filter_copy(p, d).start()
+
+    def send_lower(along_y, when=None):
+        for d in sorted(LOWER, key=lambda d: (d[0] != 0 if along_y == 0 else 0, -sum(map(abs, d)))):
+            if d[1] == along_y:
+                go = inside(d) if when is None else jnp.logical_and(inside(d), when)
+
+                @pl.when(go)
+                def _(d=d):
+                    lower_copy(d).start()
+
+    up_far, down_far = my_core == 1, my_core == 0
 
     def wait_received(p, along_y):
-        for d in DIRECTIONS:
+        for d in reversed(DIRECTIONS):
             if bool(d[1]) == along_y:
                 @pl.when(inside(tuple(-s for s in d)))
                 def _(d=d):
@@ -352,15 +366,19 @@
             target[m] = tile[m:m + 1]
 
     pl.semaphore_wait(barrier, waits)
-    for d in LOWER:
-        @pl.when(inside(d))
-        def _(d=d):
-            lower_copy(d).start()
-    send_filter(0)
-
-    def wait_lower(along_y):
+    send_filter(0, 1, up_far, (False,))
+    send_lower(-1, down_far)
+    send_filter(0, -1, down_far)
+    send_lower(0)
+    send_filter(0, 1, up_far, (True,))
+    send_filter(0, 0)
+    send_lower(-1, up_far)
+    send_filter(0, -1, up_far)
+    send_filter(0, 1, down_far)
+
+    def wait_lower(*directions):
         for d in LOWER:
-            if bool(d[1]) == along_y:
+            if d in directions:
                 @pl.when(inside(tuple(-s for s in d)))
                 def _(d=d):
                     lower_copy(d).wait_recv()
@@ -377,13 +395,11 @@
             out += [u + up, up - u]
         return out
 
-    wait_lower(False)
+    wait_lower((0, 0, -1))
     for k in range(GROUPS):
         for n, v in enumerate(z_pass(k * 128, 128, [dzr[3 * k + m] for m in range(3)])):
             for i in range(4):
                 sd[n, pl.ds((4 * k + i) * NODE_PAD, NY), :] = v[i * NY:(i + 1) * NY]
-    for n, v in enumerate(z_pass(ROWS, NY, [dxzr[m] for m in range(3)])):
-        sd[n, pl.ds(NX * NODE_PAD, NY), :] = v
 
     def yz_terms(i, t):
         base = pl.multiple_of(i * NODE_PAD, 8) + 8 * t
@@ -395,7 +411,7 @@
 
     square = lambda v: v * v
 
-    def energies(t):
+    def energies(t, first, end):
         def element(i, before):
             now = yz_terms(i, t)
             w = []
@@ -418,19 +434,22 @@
         def pair(n, before):
             return tuple(element(2 * n + 2, element(2 * n + 1, before)))
 
-        lax.fori_loop(0, NX // 2, pair, tuple(yz_terms(0, t)))
+        lax.fori_loop(first, end, pair, tuple(yz_terms(2 * first, t)))
 
     for t in range(NY // 8 - 1):
-        energies(t)
+        energies(t, 0, NX // 2 - 1)
+    wait_lower((-1, 0, 0), (-1, 0, -1))
+    for n, v in enumerate(z_pass(ROWS, NY, [dxzr[m] for m in range(3)])):
+        sd[n, pl.ds(NX * NODE_PAD, NY), :] = v
+    for t in range(NY // 8 - 1):
+        energies(t, NX // 2 - 1, NX // 2)
     add_xz(0, acc)
-    wait_lower(True)
+    wait_lower(*[d for d in LOWER if d[1]])
     for m in range(3):
         nodes[m, pl.ds(ROWS + NY + NX, 1), :] = dxyr[m]
     for n, v in enumerate(z_pass(ROWS + NY, NY, [pltpu.roll(dyzr[m] + dxyzr[m], 128 - NY, 1) for m in range(3)])):
         sd[n, pl.ds(NY, NX + 1, stride=NODE_PAD), :] = v[:NX + 1]
-    energies(NY // 8 - 1)
-
-    add_y(0, acc)
+    energies(NY // 8 - 1, 0, NX // 2)
 
     def inverse_cover(index, extent):
         end = extent - 1
@@ -440,14 +459,31 @@
     inverse_yz = inverse_cover(iota((NY, NZ), 0) + gy * NY, NY * size_y) * inverse_cover(
         iota((NY, NZ), 1) + gz * NZ, NZ * size_z)
 
+    def weigh(physical, energies_, inverse):
+        product = physical * physical * energies_
+        return -3.0 * product * inverse, physical * product
+
+    y_rows = (0, 1, NY - 2, NY - 1)
     total = jnp.zeros((NY, NZ), F32)
     for i in range(NX):
         inverse = inverse_yz * inverse_cover(gx * NX + i, NX * size_x)
-        physical = acc[pl.ds(i * NY, NY), :] * inverse
-        product = physical * physical * energy[pl.ds(i * NY, NY), :]
-        field[pl.ds((i + 2) * NY, NY), :] = -3.0 * product * inverse
-        total = total + physical * product
-    total = jnp.sum(total, axis=0, keepdims=True)
+        slope, term = weigh(acc[pl.ds(i * NY, NY), :] * inverse, energy[pl.ds(i * NY, NY), :], inverse)
+        field[pl.ds((i + 2) * NY, NY), :] = slope
+        total = total + term
+    row = iota((NY, NZ), 0)
+    inner = jnp.logical_and(row >= 2, row < NY - 2)
+    total = jnp.sum(jnp.where(inner, total, 0.0), axis=0, keepdims=True)
+
+    inverse_x = inverse_cover(iota((NX, NZ), 0) + gx * NX, NX * size_x)
+    inverses = [inverse_x * inverse_yz[row:row + 1] for row in y_rows]
+    energy_rows = [energy[pl.ds(row, NX, stride=NY), :] for row in y_rows]
+    add_y(0, acc)
+    rows_total = jnp.zeros((NX, NZ), F32)
+    for n, row in enumerate(y_rows):
+        slope, term = weigh(acc[pl.ds(row, NX, stride=NY), :] * inverses[n], energy_rows[n], inverses[n])
+        field[pl.ds(2 * NY + row, NX, stride=NY), :] = slope
+        rows_total = rows_total + term
+    total = total + jnp.sum(rows_total, axis=0, keepdims=True)
 
     def sum_copy(s, mine, to):
         return remote(part.at[s], part_in.at[s, mine], psend_sem.at[s], precv_sem.at[s], to)
@@ -463,7 +499,8 @@
         def _(z=z, c=c):
             sum_copy(0, mine, at_zc(z, c)).start()
     local_filter(1, out)
-    send_filter(1)
+    for along_y in (1, 0, -1):
+        send_filter(1, along_y)
 
     @pl.when(early)
     def _():
@@ -494,13 +531,14 @@
         sum_wait(precv_sem, 1, len(plane))
         part[2] = jnp.sum(part_in[1, 0:len(plane) + 1], axis=0)
 
-    def pass_on(z):
-        return remote(part.at[2], part_in.at[2, 0], pass_sem.at[z - layers_z], precv_sem.at[2], at_zc(z, my_core))
-
-    for z in serves:
-        @pl.when(my_z == served_from(z))
-        def _(z=z):
-            pass_on(z).start()
+    def pass_on(z, c):
+        return remote(
+            part.at[2], part_in.at[2, 0], pass_sem.at[2 * (z - layers_z) + c], precv_sem.at[2], at_zc(z, c))
+
+    for z, c in serves:
+        @pl.when(serving(z))
+        def _(z=z, c=c):
+            pass_on(z, c).start()
 
     @pl.when(jnp.logical_not(early))
     def _():
@@ -511,10 +549,10 @@
 
     total_out[...] = jnp.broadcast_to(jnp.sum(part[2], axis=1, keepdims=True), (8, 128))
 
-    for z in serves:
-        @pl.when(my_z == served_from(z))
-        def _(z=z):
-            pass_on(z).wait_send()
+    for z, c in serves:
+        @pl.when(serving(z))
+        def _(z=z, c=c):
+            pass_on(z, c).wait_send()
 
 
 def exchange(mesh, density, displacement):

time: 34.4 us -> 34.2 us (level)
  no operation moved by 1% of the time
where the time goes in v5:
time: 34.2 us; the launch traced here: 34 us
  Pallas kernels  33.4 us (98%)
  between operations  0.64 us (2%)
    pallas_call x1, Pallas kernels, exchange(): pl.pallas_call(functools.partial(kernel, sizes), out_shape=[jax.ShapeDtyp...  32.6 us
    pallas_call x1, Pallas kernels, shards(): pl.pallas_call(functools.partial(scale_kernel, float(ROWS * NZ * mesh.siz...  0.8 us

profile of v5, /device:TPU:1, one launch (start us, length us, event | category | flops | bytes accessed | tf_op | source)
XLA Modules:
  0.0 34.0 jit_solution(2141405395665973470)
XLA Ops:
  0.6 32.6 %shard_map.41 = (f32[768,128]{1,0:T(8,128)S(1)}, f32[8,128]{1,0:T(8,128)S(1)}) custom-call(f32[768,128]{1,0:T(8,128)} %bitcast.5, f32[3,768,128]{2,1,0:T(8,128)} %bitcast.4), custom_call_target="tpu_custom_call" | custom-call | flops 20000000 | bytes 2000000 | tf_op jit(solution)/shard_map/pallas_call | solution.py:574
  33.2 0.8 %shard_map.42 = (f32[768,128]{1,0:T(8,128)}, f32[1,1]{1,0:T(1,128)}) custom-call(f32[768,128]{1,0:T(8,128)S(1)} %get-tuple-element.6.field, f32[8,128]{1,0:T(8,128)S(1)} %get-tuple-element.7.total), custom_call_target="tpu_custom_call" | custom-call | tf_op jit(solution)/shard_map/pallas_call | solution.py:604

commit v6 on v5

--- a/solution.py
+++ b/solution.py
@@ -172,11 +172,11 @@
     lower = {
         (-1, 0, 0): (nodes.at[:, pl.ds(0, NY)], nodes.at[:, pl.ds(ROWS, NY)]),
         (0, -1, 0): (dys, nodes.at[:, pl.ds(ROWS + NY, NX)]),
-        (-1, -1, 0): (dxys, dxyr),
-        (0, 0, -1): (dzs, dzr),
-        (-1, 0, -1): (dxzs, dxzr),
-        (0, -1, -1): (dyzs, dyzr),
-        (-1, -1, -1): (dxyzs, dxyzr),
+        (-1, -1, 0): (dxys.at[pl.ds(0, 3)], dxyr.at[pl.ds(0, 3)]),
+        (0, 0, -1): (dzs.at[pl.ds(0, 3 * GROUPS)], dzr.at[pl.ds(0, 3 * GROUPS)]),
+        (-1, 0, -1): (dxzs.at[pl.ds(0, 3)], dxzr.at[pl.ds(0, 3)]),
+        (0, -1, -1): (dyzs.at[pl.ds(0, 3)], dyzr.at[pl.ds(0, 3)]),
+        (-1, -1, -1): (dxyzs.at[pl.ds(0, 3)], dxyzr.at[pl.ds(0, 3)]),
     }
 
     for d in DIRECTIONS:
@@ -562,13 +562,13 @@
     scratch = [
         vmem((NX + 4) * NY, NZ), vmem(NX * YPAD, NZ), vmem(4 * YPAD, NZ), vmem(ROWS, NZ),
         vmem(128, NZ), vmem(128, NZ), vmem(3, ROWS + 2 * NY, NZ),
-        vmem(6, (NX + 1) * NODE_PAD, NZ), vmem(ROWS, NZ)]
-    filters = [vmem(2, 2, 2 * NY, NZ), vmem(2, 2, 2, NX, NZ), vmem(2, 2, 2, 4, 1, NZ), vmem(2, 2, 2 * GROUPS, 1, 128),
-               vmem(2, 2, 2, 2, 1, 128), vmem(2, 2, 2, 2, 1, 128), vmem(2, 2, 2, 2, 2, 1, 128)]
+        vmem(6, 32 * NODE_PAD, NZ), vmem(ROWS, NZ)]
+    filters = [vmem(2, 2, 2 * NY, NZ), vmem(2, 2, 2, NX, NZ), vmem(3, 2, 2, 4, 1, NZ), vmem(3, 2, 2 * GROUPS, 1, 128),
+               vmem(3, 2, 2, 2, 1, 128), vmem(3, 2, 2, 2, 1, 128), vmem(3, 2, 2, 2, 2, 1, 128)]
     scratch += filters + filters
-    edges = [vmem(3, 1, NZ), vmem(3 * GROUPS, 1, 128), vmem(3, 1, 128), vmem(3, 1, 128), vmem(3, 1, 128)]
+    edges = [vmem(11, 1, NZ), vmem(3 * GROUPS + 8, 1, 128), vmem(11, 1, 128), vmem(11, 1, 128), vmem(11, 1, 128)]
     scratch += [vmem(3, NX, NZ)] + edges + edges + [vmem(128, 128)]
-    scratch += [vmem(3, 1, 128), vmem(3, partners, 1, 128)]
+    scratch += [vmem(11, 1, 128), vmem(4, partners, 1, 128)]
     dma = pltpu.SemaphoreType.DMA
     scratch += [dma((2, 27)), dma((2, 27)), dma((8,)), dma((8,)), dma((2,)), dma((3,)), dma((3,)), dma((8,))]
     return pl.pallas_call(

time: 34.2 us -> 34.2 us (level)
  no operation moved by 1% of the time
where the time goes in v6:
time: 34.2 us; the launch traced here: 34 us
  Pallas kernels  33.4 us (98%)
  between operations  0.64 us (2%)
    pallas_call x1, Pallas kernels, exchange(): pl.pallas_call(functools.partial(kernel, sizes), out_shape=[jax.ShapeDtyp...  32.6 us
    pallas_call x1, Pallas kernels, shards(): pl.pallas_call(functools.partial(scale_kernel, float(ROWS * NZ * mesh.siz...  0.8 us

profile of v6, /device:TPU:1, one launch (start us, length us, event | category | flops | bytes accessed | tf_op | source)
XLA Modules:
  0.0 34.0 jit_solution(14169469953758620580)
XLA Ops:
  0.6 32.6 %shard_map.41 = (f32[768,128]{1,0:T(8,128)S(1)}, f32[8,128]{1,0:T(8,128)S(1)}) custom-call(f32[768,128]{1,0:T(8,128)} %bitcast.5, f32[3,768,128]{2,1,0:T(8,128)} %bitcast.4), custom_call_target="tpu_custom_call" | custom-call | flops 20000000 | bytes 2000000 | tf_op jit(solution)/shard_map/pallas_call | solution.py:574
  33.2 0.8 %shard_map.42 = (f32[768,128]{1,0:T(8,128)}, f32[1,1]{1,0:T(1,128)}) custom-call(f32[768,128]{1,0:T(8,128)S(1)} %get-tuple-element.6.field, f32[8,128]{1,0:T(8,128)S(1)} %get-tuple-element.7.total), custom_call_target="tpu_custom_call" | custom-call | tf_op jit(solution)/shard_map/pallas_call | solution.py:604

commit v7 on v6

--- a/solution.py
+++ b/solution.py
@@ -293,9 +293,9 @@
 
     up_far, down_far = my_core == 1, my_core == 0
 
-    def wait_received(p, along_y):
+    def wait_received(p, along_y, along_z=(False, True)):
         for d in reversed(DIRECTIONS):
-            if bool(d[1]) == along_y:
+            if bool(d[1]) == along_y and bool(d[2]) in along_z:
                 @pl.when(inside(tuple(-s for s in d)))
                 def _(d=d):
                     filter_copy(p, d).wait_recv()
@@ -319,10 +319,7 @@
             acc[pl.ds(k * 128, 128), :] = acc[pl.ds(k * 128, 128), :] + z_edges(low, high)
 
     def add_y(p, acc):
-        wait_received(p, True)
-        low, high = [[sum([yzr[p, sy, sz, i] for sy in range(2)] + [
-            xyzr[p, sx, sy, sz, i] for sx in range(2) for sy in range(2)]) for i in range(2)] for sz in (1, 0)]
-        turned = z_edges(low, high)
+        wait_received(p, True, (False,))
         at = {}
         for sy in range(2):
             for n in range(2):
@@ -334,7 +331,14 @@
         for n, (row, v) in enumerate((
                 (0, at[1, 0] + 2.0 * at[1, 1]), (1, at[1, 1]), (NY - 2, at[0, 0]), (NY - 1, 2.0 * at[0, 0] + at[0, 1]))):
             place = pl.ds(row, NX, stride=NY)
-            acc[place, :] = acc[place, :] + v + turned[n * 32:n * 32 + NX]
+            acc[place, :] = acc[place, :] + v
+        wait_received(p, True, (True,))
+        low, high = [[sum([yzr[p, sy, sz, i] for sy in range(2)] + [
+            xyzr[p, sx, sy, sz, i] for sx in range(2) for sy in range(2)]) for i in range(2)] for sz in (1, 0)]
+        turned = z_edges(low, high)
+        for n, row in enumerate((0, 1, NY - 2, NY - 1)):
+            place = pl.ds(row, NX, stride=NY)
+            acc[place, :] = acc[place, :] + turned[n * 32:n * 32 + NX]
 
     load_density.wait()
     local_filter(0, acc)

time: 34.2 us -> 34.2 us (level)
  no operation moved by 1% of the time
where the time goes in v7:
time: 34.2 us; the launch traced here: 34 us
  Pallas kernels  33.4 us (98%)
  between operations  0.64 us (2%)
    pallas_call x1, Pallas kernels, exchange(): pl.pallas_call(functools.partial(kernel, sizes), out_shape=[jax.ShapeDtyp...  32.6 us
    pallas_call x1, Pallas kernels, shards(): pl.pallas_call(functools.partial(scale_kernel, float(ROWS * NZ * mesh.siz...  0.8 us

profile of v7, /device:TPU:1, one launch (start us, length us, event | category | flops | bytes accessed | tf_op | source)
XLA Modules:
  0.0 34.0 jit_solution(9420820025015708709)
XLA Ops:
  0.6 32.6 %shard_map.41 = (f32[768,128]{1,0:T(8,128)S(1)}, f32[8,128]{1,0:T(8,128)S(1)}) custom-call(f32[768,128]{1,0:T(8,128)} %bitcast.5, f32[3,768,128]{2,1,0:T(8,128)} %bitcast.4), custom_call_target="tpu_custom_call" | custom-call | flops 20000000 | bytes 2000000 | tf_op jit(solution)/shard_map/pallas_call | solution.py:578
  33.2 0.8 %shard_map.42 = (f32[768,128]{1,0:T(8,128)}, f32[1,1]{1,0:T(1,128)}) custom-call(f32[768,128]{1,0:T(8,128)S(1)} %get-tuple-element.6.field, f32[8,128]{1,0:T(8,128)S(1)} %get-tuple-element.7.total), custom_call_target="tpu_custom_call" | custom-call | tf_op jit(solution)/shard_map/pallas_call | solution.py:608
